TPU v7x, 32 devices: a whole 2x2x4 slice. The times are simulated.
32 devices in a mesh: seq: 8 (over y, x, core), head: 4 (over z).
Axes of the slice: x: 2, y: 2, z: 4, core: 2. Of those that a mesh axis runs over, the one named last changes fastest.
Arguments:
- query: bfloat16 [4096, 7168], P(('seq', 'head')), may hold values from -16 to 16
- key: bfloat16 [4096, 7168], P(('seq', 'head')), may hold values from -16 to 16
- value: bfloat16 [4096, 7168], P(('seq', 'head')), may hold values from -8 to 8
- exponent: int32 [64], replicated, may hold values from 1 to 64, as said below
Outputs:
- attended: bfloat16 [4096, 7168], P(('seq', 'head'))
Inputs may be any that keep to these rules, and one draw needn't show every extreme that they name: Head h (counted from 0) has an exponent within 6 of h + 1; head 0 has 1 and the last head has 64.
All inputs are finite; a program needn't handle non-finite values.
Results may differ from a plain program's by a relative error of at most 0.0033.
Values may be sent and summed in bfloat16 or wider, within the bound.
No kernel may reach another device: no remote copies, remote signals or barrier semaphores. Data moves between devices by JAX's collectives and lax.ppermute only.
A program may use at most 128 MiB of HBM per device.

v0:
```python
import jax
import jax.numpy as jnp
from jax import lax
from jax.sharding import PartitionSpec as P

BLOCK = 128
MIN_BAND = 16
MAX_BAND = 40


masked_score = -1e30


def passed_along(x, axis, by):
    length = lax.axis_size(axis)
    pairs = [(i, i + by) for i in range(length) if 0 <= i + by < length]
    return lax.ppermute(x, axis, pairs)


def attend_rows(
    query_block,
    keys_head,
    values_head,
    query_first,
    anchor,
    tile_low,
    tile_high,
    head_slope,
    head_band,
):
    block_rows, head_width = query_block.shape
    factor = head_width ** (-0.5)
    query_pos = query_first + jnp.arange(block_rows, dtype=jnp.int32)

    def tile_step(tile, state):
        running_max, weight_sum, accum = state
        tile_start = tile * block_rows
        key_tile = lax.dynamic_slice_in_dim(keys_head, tile_start, block_rows, 0)
        value_tile = lax.dynamic_slice_in_dim(values_head, tile_start, block_rows, 0)
        key_pos = anchor + tile_start + jnp.arange(block_rows, dtype=jnp.int32)
        distance = query_pos[:, None] - key_pos[None, :]
        scores = (
            lax.dot_general(
                query_block, key_tile, (((1,), (1,)), ((), ())), preferred_element_type=jnp.float32
            )
            * factor
        )
        scores = scores - head_slope * distance.astype(jnp.float32)
        live = (
            (key_pos[None, :] >= 0)
            & (distance >= 0)
            & (query_pos[:, None] // BLOCK - key_pos[None, :] // BLOCK < head_band)
        )
        scores = jnp.where(live, scores, masked_score)
        new_max = jnp.maximum(running_max, jnp.max(scores, axis=1, keepdims=True))
        weights = jnp.where(live, jnp.exp(scores - new_max), 0.0)
        shrink = jnp.exp(running_max - new_max)
        weight_sum = weight_sum * shrink + jnp.sum(weights, axis=1, keepdims=True)
        accum = accum * shrink + jnp.dot(
            weights.astype(jnp.bfloat16), value_tile, preferred_element_type=jnp.float32
        )
        return (new_max, weight_sum, accum)

    start_state = (
        jnp.full((block_rows, 1), masked_score, jnp.float32),
        jnp.zeros((block_rows, 1), jnp.float32),
        jnp.zeros((block_rows, head_width), jnp.float32),
    )
    final_state = lax.fori_loop(tile_low, tile_high + 1, tile_step, start_state)
    return (final_state[2] / final_state[1]).astype(jnp.bfloat16)


def on_device(query, key, value, exponent):
    token_rows, width_total = query.shape
    heads_total = exponent.shape[0]
    head_width = width_total // heads_total
    group_count = lax.axis_size("seq")
    slot_count = lax.axis_size("head")
    local_heads = heads_total // slot_count
    group_rows = token_rows * slot_count
    group_id = lax.axis_index("seq")
    slot_id = lax.axis_index("head")
    band_list = MIN_BAND + (exponent - 1) * (MAX_BAND - MIN_BAND) // (heads_total - 1)
    query_in, key_in, value_in = (query, key, value)
    head_ids = slot_id * local_heads + jnp.arange(local_heads, dtype=jnp.int32)
    local_exponent = jnp.take(exponent, head_ids)
    local_slopes = jnp.exp2(-12.0 * local_exponent.astype(jnp.float32) / heads_total)
    local_bands = jnp.take(band_list, head_ids)
    query_group, key_group, value_group = (
        lax.all_to_all(query_in, "head", split_axis=1, concat_axis=0, tiled=True),
        lax.all_to_all(key_in, "head", split_axis=1, concat_axis=0, tiled=True),
        lax.all_to_all(value_in, "head", split_axis=1, concat_axis=0, tiled=True),
    )
    local_width = query_group.shape[1]
    reach = min(((MAX_BAND - 1) * BLOCK + group_rows - 1) // group_rows, group_count - 1)
    key_pieces = []
    value_pieces = []
    for distance in range(1, reach + 1):
        moved_key, moved_value = passed_along((key_group, value_group), "seq", distance)
        key_pieces.insert(0, moved_key)
        value_pieces.insert(0, moved_value)
    keys_all = jnp.concatenate(key_pieces + [key_group], axis=0)
    values_all = jnp.concatenate(value_pieces + [value_group], axis=0)
    anchor = (group_id - reach) * group_rows
    query_rows = min(512, group_rows)

    def head_step(head_pos, out_buffer):
        column = head_pos * head_width
        query_head = lax.dynamic_slice_in_dim(query_group, column, head_width, 1)
        keys_head = lax.dynamic_slice_in_dim(keys_all, column, head_width, 1)
        values_head = lax.dynamic_slice_in_dim(values_all, column, head_width, 1)
        head_slope = local_slopes[head_pos]
        head_band = local_bands[head_pos]
        results = []
        for block_id in range(group_rows // query_rows):
            query_first = group_id * group_rows + block_id * query_rows
            first_block = query_first // BLOCK - (head_band - 1)
            lowest = jnp.maximum(jnp.maximum(first_block * BLOCK, 0) - anchor, 0)
            tile_low = lowest // query_rows
            tile_high = (reach * group_rows + block_id * query_rows) // query_rows
            query_block = query_head[block_id * query_rows : (block_id + 1) * query_rows]
            results.append(
                attend_rows(
                    query_block,
                    keys_head,
                    values_head,
                    query_first,
                    anchor,
                    tile_low,
                    tile_high,
                    head_slope,
                    head_band,
                )
            )
        head_result = jnp.concatenate(results, axis=0)
        return lax.dynamic_update_slice_in_dim(out_buffer, head_result, column, 1)

    attended_group = lax.fori_loop(
        0, local_heads, head_step, jnp.zeros((group_rows, local_width), jnp.bfloat16)
    )
    returned = lax.all_to_all(attended_group, "head", split_axis=0, concat_axis=1, tiled=True)
    return returned


def solution(mesh):
    return jax.shard_map(
        on_device,
        mesh=mesh,
        in_specs=(
            P(("seq", "head"), None),
            P(("seq", "head"), None),
            P(("seq", "head"), None),
            P(),
        ),
        out_specs=P(("seq", "head"), None),
        check_vma=False,
    )
```

profile of v0, /device:TPU:7, one launch (start us, length us, event | category | flops | bytes accessed | tf_op | source)
XLA Modules:
  0.0 1109.7 jit_solution(1537707565200990752)
XLA Ops:
  2.9 4.6 all-to-all-start.1
  10.3 39.2 %all-to-all-done.1 = bf16[128,4,1792]{2,0,1:T(8,128)(2,1)S(1)} async-done(((bf16[128,4,1792]{2,0,1:T(8,128)(2,1)}), bf16[128,4,1792]{2,0,1:T(8,128)(2,1)S(1)}, u32[]{:S(2)}, u32[]{:S(2)}) %all-to-all-start.1) | async-done | bytes 1835040 | tf_op jit(solution)/shard_map/all_to_all | solution.py:92
  61.0 38.3 %collective-permute-done.7 = bf16[512,1792]{1,0:T(8,128)(2,1)} collective-permute-done((bf16[512,1792]{1,0:T(8,128)(2,1)}, bf16[512,1792]{1,0:T(8,128)(2,1)}, u32[]{:S(2)}, u32[]{:S(2)}) %collective-permute-start.7) | collective-permute-done | bytes 1835040 | tf_op jit(solution)/shard_map/ppermute | solution.py:17
  110.6 67.9 %collective-permute-done.9 = bf16[512,1792]{1,0:T(8,128)(2,1)} collective-permute-done((bf16[512,1792]{1,0:T(8,128)(2,1)}, bf16[512,1792]{1,0:T(8,128)(2,1)}, u32[]{:S(2)}, u32[]{:S(2)}) %collective-permute-start.9) | collective-permute-done | bytes 1835040 | tf_op jit(solution)/shard_map/ppermute | solution.py:17
  194.8 61.7 %collective-permute-done = bf16[512,1792]{1,0:T(8,128)(2,1)S(1)} collective-permute-done((bf16[512,1792]{1,0:T(8,128)(2,1)S(1)}, bf16[512,1792]{1,0:T(8,128)(2,1)S(1)}, u32[]{:S(2)}, u32[]{:S(2)}) %collective-permute-start) | collective-permute-done | bytes 1835040 | tf_op jit(solution)/shard_map/ppermute | solution.py:17
  264.2 72.0 %collective-permute-done.2 = bf16[512,1792]{1,0:T(8,128)(2,1)S(1)} collective-permute-done((bf16[512,1792]{1,0:T(8,128)(2,1)S(1)}, bf16[512,1792]{1,0:T(8,128)(2,1)S(1)}, u32[]{:S(2)}, u32[]{:S(2)}) %collective-permute-start.2) | collective-permute-done | bytes 1835040 | tf_op jit(solution)/shard_map/ppermute | solution.py:17
  345.8 543.9 %while.64 = (s32[]{:T(128)}, bf16[512,1792]{0,1:T(8,128)(2,1)}, s32[16]{0:T(128)S(1)}, s32[]{:T(128)}, s32[]{:T(128)}, /*index=5*/bf16[4096,1792]{1,0:T(8,128)(2...) while((s32[]{:T(128)}, bf16[512,1792]{0,1:T(8,128)(2,1)}, ...), condition=%wide.region_5.7_spmd, body=%wide.region_0.6_spmd.sunk | while | flops 125553688 | bytes 8550196 | solution.py:138
  351.9 24.2 %while.65 = (s32[]{:T(128)}, f32[512,1]{0,1:T(1,128)S(1)}, f32[512,1]{0,1:T(1,128)S(1)}, f32[512,112]{0,1:T(8,128)S(1)}, s32[]{:T(128)}, /*index=5*/s32[]{:T(128...) while((s32[]{:T(128)}, f32[512,1]{0,1:T(1,128)S(1)}, ...), condition=%wide.region_4.5_spmd.clone.clone, body=%wide.region_1.4_spmd.clone.clone.sunk | while | flops 125438984 | bytes 4070643 | solution.py:69
  382.9 24.2 %while.65 = (s32[]{:T(128)}, f32[512,1]{0,1:T(1,128)S(1)}, f32[512,1]{0,1:T(1,128)S(1)}, f32[512,112]{0,1:T(8,128)S(1)}, s32[]{:T(128)}, /*index=5*/s32[]{:T(128...) while((s32[]{:T(128)}, f32[512,1]{0,1:T(1,128)S(1)}, ...), condition=%wide.region_4.5_spmd.clone.clone, body=%wide.region_1.4_spmd.clone.clone.sunk | while | flops 125438984 | bytes 4070643 | solution.py:69
  413.9 24.2 %while.65 = (s32[]{:T(128)}, f32[512,1]{0,1:T(1,128)S(1)}, f32[512,1]{0,1:T(1,128)S(1)}, f32[512,112]{0,1:T(8,128)S(1)}, s32[]{:T(128)}, /*index=5*/s32[]{:T(128...) while((s32[]{:T(128)}, f32[512,1]{0,1:T(1,128)S(1)}, ...), condition=%wide.region_4.5_spmd.clone.clone, body=%wide.region_1.4_spmd.clone.clone.sunk | while | flops 125438984 | bytes 4070643 | solution.py:69
  444.9 24.2 %while.65 = (s32[]{:T(128)}, f32[512,1]{0,1:T(1,128)S(1)}, f32[512,1]{0,1:T(1,128)S(1)}, f32[512,112]{0,1:T(8,128)S(1)}, s32[]{:T(128)}, /*index=5*/s32[]{:T(128...) while((s32[]{:T(128)}, f32[512,1]{0,1:T(1,128)S(1)}, ...), condition=%wide.region_4.5_spmd.clone.clone, body=%wide.region_1.4_spmd.clone.clone.sunk | while | flops 125438984 | bytes 4070643 | solution.py:69
  476.0 29.0 %while.65 = (s32[]{:T(128)}, f32[512,1]{0,1:T(1,128)S(1)}, f32[512,1]{0,1:T(1,128)S(1)}, f32[512,112]{0,1:T(8,128)S(1)}, s32[]{:T(128)}, /*index=5*/s32[]{:T(128...) while((s32[]{:T(128)}, f32[512,1]{0,1:T(1,128)S(1)}, ...), condition=%wide.region_4.5_spmd.clone.clone, body=%wide.region_1.4_spmd.clone.clone.sunk | while | flops 125438984 | bytes 4070643 | solution.py:69
  511.8 24.2 %while.65 = (s32[]{:T(128)}, f32[512,1]{0,1:T(1,128)S(1)}, f32[512,1]{0,1:T(1,128)S(1)}, f32[512,112]{0,1:T(8,128)S(1)}, s32[]{:T(128)}, /*index=5*/s32[]{:T(128...) while((s32[]{:T(128)}, f32[512,1]{0,1:T(1,128)S(1)}, ...), condition=%wide.region_4.5_spmd.clone.clone, body=%wide.region_1.4_spmd.clone.clone.sunk | while | flops 125438984 | bytes 4070643 | solution.py:69
  542.8 29.0 %while.65 = (s32[]{:T(128)}, f32[512,1]{0,1:T(1,128)S(1)}, f32[512,1]{0,1:T(1,128)S(1)}, f32[512,112]{0,1:T(8,128)S(1)}, s32[]{:T(128)}, /*index=5*/s32[]{:T(128...) while((s32[]{:T(128)}, f32[512,1]{0,1:T(1,128)S(1)}, ...), condition=%wide.region_4.5_spmd.clone.clone, body=%wide.region_1.4_spmd.clone.clone.sunk | while | flops 125438984 | bytes 4070643 | solution.py:69
  578.7 24.2 %while.65 = (s32[]{:T(128)}, f32[512,1]{0,1:T(1,128)S(1)}, f32[512,1]{0,1:T(1,128)S(1)}, f32[512,112]{0,1:T(8,128)S(1)}, s32[]{:T(128)}, /*index=5*/s32[]{:T(128...) while((s32[]{:T(128)}, f32[512,1]{0,1:T(1,128)S(1)}, ...), condition=%wide.region_4.5_spmd.clone.clone, body=%wide.region_1.4_spmd.clone.clone.sunk | while | flops 125438984 | bytes 4070643 | solution.py:69
  609.7 24.2 %while.65 = (s32[]{:T(128)}, f32[512,1]{0,1:T(1,128)S(1)}, f32[512,1]{0,1:T(1,128)S(1)}, f32[512,112]{0,1:T(8,128)S(1)}, s32[]{:T(128)}, /*index=5*/s32[]{:T(128...) while((s32[]{:T(128)}, f32[512,1]{0,1:T(1,128)S(1)}, ...), condition=%wide.region_4.5_spmd.clone.clone, body=%wide.region_1.4_spmd.clone.clone.sunk | while | flops 125438984 | bytes 4070643 | solution.py:69
  640.7 24.2 %while.65 = (s32[]{:T(128)}, f32[512,1]{0,1:T(1,128)S(1)}, f32[512,1]{0,1:T(1,128)S(1)}, f32[512,112]{0,1:T(8,128)S(1)}, s32[]{:T(128)}, /*index=5*/s32[]{:T(128...) while((s32[]{:T(128)}, f32[512,1]{0,1:T(1,128)S(1)}, ...), condition=%wide.region_4.5_spmd.clone.clone, body=%wide.region_1.4_spmd.clone.clone.sunk | while | flops 125438984 | bytes 4070643 | solution.py:69
  671.7 29.0 %while.65 = (s32[]{:T(128)}, f32[512,1]{0,1:T(1,128)S(1)}, f32[512,1]{0,1:T(1,128)S(1)}, f32[512,112]{0,1:T(8,128)S(1)}, s32[]{:T(128)}, /*index=5*/s32[]{:T(128...) while((s32[]{:T(128)}, f32[512,1]{0,1:T(1,128)S(1)}, ...), condition=%wide.region_4.5_spmd.clone.clone, body=%wide.region_1.4_spmd.clone.clone.sunk | while | flops 125438984 | bytes 4070643 | solution.py:69
  707.6 33.9 %while.65 = (s32[]{:T(128)}, f32[512,1]{0,1:T(1,128)S(1)}, f32[512,1]{0,1:T(1,128)S(1)}, f32[512,112]{0,1:T(8,128)S(1)}, s32[]{:T(128)}, /*index=5*/s32[]{:T(128...) while((s32[]{:T(128)}, f32[512,1]{0,1:T(1,128)S(1)}, ...), condition=%wide.region_4.5_spmd.clone.clone, body=%wide.region_1.4_spmd.clone.clone.sunk | while | flops 125438984 | bytes 4070643 | solution.py:69
  748.3 29.0 %while.65 = (s32[]{:T(128)}, f32[512,1]{0,1:T(1,128)S(1)}, f32[512,1]{0,1:T(1,128)S(1)}, f32[512,112]{0,1:T(8,128)S(1)}, s32[]{:T(128)}, /*index=5*/s32[]{:T(128...) while((s32[]{:T(128)}, f32[512,1]{0,1:T(1,128)S(1)}, ...), condition=%wide.region_4.5_spmd.clone.clone, body=%wide.region_1.4_spmd.clone.clone.sunk | while | flops 125438984 | bytes 4070643 | solution.py:69
  784.1 29.0 %while.65 = (s32[]{:T(128)}, f32[512,1]{0,1:T(1,128)S(1)}, f32[512,1]{0,1:T(1,128)S(1)}, f32[512,112]{0,1:T(8,128)S(1)}, s32[]{:T(128)}, /*index=5*/s32[]{:T(128...) while((s32[]{:T(128)}, f32[512,1]{0,1:T(1,128)S(1)}, ...), condition=%wide.region_4.5_spmd.clone.clone, body=%wide.region_1.4_spmd.clone.clone.sunk | while | flops 125438984 | bytes 4070643 | solution.py:69
  820.0 29.0 %while.65 = (s32[]{:T(128)}, f32[512,1]{0,1:T(1,128)S(1)}, f32[512,1]{0,1:T(1,128)S(1)}, f32[512,112]{0,1:T(8,128)S(1)}, s32[]{:T(128)}, /*index=5*/s32[]{:T(128...) while((s32[]{:T(128)}, f32[512,1]{0,1:T(1,128)S(1)}, ...), condition=%wide.region_4.5_spmd.clone.clone, body=%wide.region_1.4_spmd.clone.clone.sunk | while | flops 125438984 | bytes 4070643 | solution.py:69
  855.1 33.9 %while.65 = (s32[]{:T(128)}, f32[512,1]{0,1:T(1,128)S(1)}, f32[512,1]{0,1:T(1,128)S(1)}, f32[512,112]{0,1:T(8,128)S(1)}, s32[]{:T(128)}, /*index=5*/s32[]{:T(128...) while((s32[]{:T(128)}, f32[512,1]{0,1:T(1,128)S(1)}, ...), condition=%wide.region_4.5_spmd.clone.clone, body=%wide.region_1.4_spmd.clone.clone.sunk | while | flops 125438984 | bytes 4070643 | solution.py:69
  892.5 211.4 %all_to_all.76 = bf16[4,128,1792]{2,1,0:T(8,128)(2,1)} all-to-all(bf16[4,128,1792]{2,1,0:T(8,128)(2,1)S(1)} %bitcast.79), channel_id=1, replica_groups=mesh['seq'=8,'head'=4] {'head'}, dimensions={0} | all-to-all | bytes 3670016 | tf_op jit(solution)/shard_map/all_to_all | solution.py:141
  (1184 shorter events, 594.7 us)
Async XLA Ops:
  2.9 46.7 %all-to-all-start.1 = ((bf16[128,4,1792]{2,0,1:T(8,128)(2,1)}), bf16[128,4,1792]{2,0,1:T(8,128)(2,1)S(1)}, u32[]{:S(2)}, u32[]{:S(2)}) async-start(bf16[128,4,1792]{2,0,1:T(8,128)(2,1)} %bitcast.78), calls=%async_computation.1 | async-start | bytes 3670016 | tf_op jit(solution)/shard_map/all_to_all | solution.py:92
  49.6 1.3 copy-start.1
  49.6 51.0 %copy-start = (s32[64]{0:T(128)S(1)}, s32[64]{0:T(128)}, u32[]{:S(2)}) copy-start(s32[64]{0:T(128)} %param.13) | copy-start | bytes 772
  50.9 55.3 %all-to-all-start = ((bf16[128,4,1792]{2,0,1:T(8,128)(2,1)}), bf16[128,4,1792]{2,0,1:T(8,128)(2,1)S(1)}, u32[]{:S(2)}, u32[]{:S(2)}) async-start(bf16[128,4,1792]{2,0,1:T(8,128)(2,1)} %bitcast.77), calls=%async_computation | async-start | bytes 3670016 | tf_op jit(solution)/shard_map/all_to_all | solution.py:91
  54.4 44.8 %collective-permute-start.7 = (bf16[512,1792]{1,0:T(8,128)(2,1)}, bf16[512,1792]{1,0:T(8,128)(2,1)}, u32[]{:S(2)}, u32[]{:S(2)}) collective-permute-start(bf16[512,1792]{1,0:T(8,128)(2,1)} %bitcast.68), channel_id=1, source_target_pairs={{0,28},{1,29},{2,30},{3,31}} | collective-permute-start | bytes 5505032 | tf_op jit(solution)/shard_map/ppermute | solution.py:17
  55.7 46.2 %collective-permute-start.8 = (bf16[512,1792]{1,0:T(8,128)(2,1)}, bf16[512,1792]{1,0:T(8,128)(2,1)}, u32[]{:S(2)}, u32[]{:S(2)}) collective-permute-start(bf16[512,1792]{1,0:T(8,128)(2,1)} %bitcast.69), channel_id=1, source_target_pairs={{0,24},{4,28},{1,25},{5,29},{2,26},{6,30},{3,27},{7,31}} | collective-permute-start | bytes 5505032 | tf_op jit(solution)/shard_map/ppermute | solution.py:17
  57.0 121.4 %collective-permute-start.9 = (bf16[512,1792]{1,0:T(8,128)(2,1)}, bf16[512,1792]{1,0:T(8,128)(2,1)}, u32[]{:S(2)}, u32[]{:S(2)}) collective-permute-start(bf16[512,1792]{1,0:T(8,128)(2,1)} %bitcast.70), channel_id=1, source_target_pairs={{0,20},{4,24},{8,28},{1,21},{5,25},{9,29},{2,22},{6,26},{10,30},{3... | collective-permute-start | bytes 5505032 | tf_op jit(solution)/shard_map/ppermute | solution.py:17
  58.3 121.5 %collective-permute-start.10 = (bf16[512,1792]{1,0:T(8,128)(2,1)}, bf16[512,1792]{1,0:T(8,128)(2,1)}, u32[]{:S(2)}, u32[]{:S(2)}) collective-permute-start(bf16[512,1792]{1,0:T(8,128)(2,1)} %bitcast.71), channel_id=1, source_target_pairs={{0,16},{4,20},{8,24},{12,28},{1,17},{5,21},{9,25},{13,29},{2,18},{... | collective-permute-start | bytes 5505032 | tf_op jit(solution)/shard_map/ppermute | solution.py:17
  59.6 126.3 %collective-permute-start.11 = (bf16[512,1792]{1,0:T(8,128)(2,1)}, bf16[512,1792]{1,0:T(8,128)(2,1)}, u32[]{:S(2)}, u32[]{:S(2)}) collective-permute-start(bf16[512,1792]{1,0:T(8,128)(2,1)} %bitcast.72), channel_id=1, source_target_pairs={{0,12},{4,16},{8,20},{12,24},{16,28},{1,13},{5,17},{9,21},{13,25},... | collective-permute-start | bytes 5505032 | tf_op jit(solution)/shard_map/ppermute | solution.py:17
  99.3 89.6 %collective-permute-start.12 = (bf16[512,1792]{1,0:T(8,128)(2,1)}, bf16[512,1792]{1,0:T(8,128)(2,1)}, u32[]{:S(2)}, u32[]{:S(2)}) collective-permute-start(bf16[512,1792]{1,0:T(8,128)(2,1)} %bitcast.73), channel_id=1, source_target_pairs={{0,8},{4,12},{8,16},{12,20},{16,24},{20,28},{1,9},{5,13},{9,17},{1... | collective-permute-start | bytes 5505032 | tf_op jit(solution)/shard_map/ppermute | solution.py:17
  102.0 89.9 %collective-permute-start.13 = (bf16[512,1792]{1,0:T(8,128)(2,1)}, bf16[512,1792]{1,0:T(8,128)(2,1)}, u32[]{:S(2)}, u32[]{:S(2)}) collective-permute-start(bf16[512,1792]{1,0:T(8,128)(2,1)} %bitcast.74), channel_id=1, source_target_pairs={{0,4},{4,8},{8,12},{12,16},{16,20},{20,24},{24,28},{1,5},{5,9},{9,... | collective-permute-start | bytes 5505032 | tf_op jit(solution)/shard_map/ppermute | solution.py:17
  106.1 238.3 %all-to-all-start.2 = ((bf16[128,4,1792]{2,0,1:T(8,128)(2,1)}), bf16[128,4,1792]{2,0,1:T(8,128)(2,1)}, u32[]{:S(2)}, u32[]{:S(2)}) async-start(bf16[128,4,1792]{2,0,1:T(8,128)(2,1)} %bitcast.76), calls=%async_computation.2 | async-start | bytes 3670016 | tf_op jit(solution)/shard_map/all_to_all | solution.py:90
  178.5 78.0 %collective-permute-start = (bf16[512,1792]{1,0:T(8,128)(2,1)S(1)}, bf16[512,1792]{1,0:T(8,128)(2,1)S(1)}, u32[]{:S(2)}, u32[]{:S(2)}) collective-permute-start(bf16[512,1792]{1,0:T(8,128)(2,1)S(1)} %bitcast.60), channel_id=1, source_target_pairs={{0,28},{1,29},{2,30},{3,31}} | collective-permute-start | bytes 5505032 | tf_op jit(solution)/shard_map/ppermute | solution.py:17
  179.8 79.6 %collective-permute-start.1 = (bf16[512,1792]{1,0:T(8,128)(2,1)S(1)}, bf16[512,1792]{1,0:T(8,128)(2,1)S(1)}, u32[]{:S(2)}, u32[]{:S(2)}) collective-permute-start(bf16[512,1792]{1,0:T(8,128)(2,1)S(1)} %bitcast.61), channel_id=1, source_target_pairs={{0,24},{4,28},{1,25},{5,29},{2,26},{6,30},{3,27},{7,31}} | collective-permute-start | bytes 5505032 | tf_op jit(solution)/shard_map/ppermute | solution.py:17
  186.0 150.2 %collective-permute-start.2 = (bf16[512,1792]{1,0:T(8,128)(2,1)S(1)}, bf16[512,1792]{1,0:T(8,128)(2,1)S(1)}, u32[]{:S(2)}, u32[]{:S(2)}) collective-permute-start(bf16[512,1792]{1,0:T(8,128)(2,1)S(1)} %bitcast.62), channel_id=1, source_target_pairs={{0,20},{4,24},{8,28},{1,21},{5,25},{9,29},{2,22},{6,26},{10,30},{3... | collective-permute-start | bytes 5505032 | tf_op jit(solution)/shard_map/ppermute | solution.py:17
  188.9 148.6 %collective-permute-start.3 = (bf16[512,1792]{1,0:T(8,128)(2,1)S(1)}, bf16[512,1792]{1,0:T(8,128)(2,1)S(1)}, u32[]{:S(2)}, u32[]{:S(2)}) collective-permute-start(bf16[512,1792]{1,0:T(8,128)(2,1)S(1)} %bitcast.63), channel_id=1, source_target_pairs={{0,16},{4,20},{8,24},{12,28},{1,17},{5,21},{9,25},{13,29},{2,18},{... | collective-permute-start | bytes 5505032 | tf_op jit(solution)/shard_map/ppermute | solution.py:17
  191.8 147.0 %collective-permute-start.4 = (bf16[512,1792]{1,0:T(8,128)(2,1)S(1)}, bf16[512,1792]{1,0:T(8,128)(2,1)S(1)}, u32[]{:S(2)}, u32[]{:S(2)}) collective-permute-start(bf16[512,1792]{1,0:T(8,128)(2,1)S(1)} %bitcast.64), channel_id=1, source_target_pairs={{0,12},{4,16},{8,20},{12,24},{16,28},{1,13},{5,17},{9,21},{13,25},... | collective-permute-start | bytes 5505032 | tf_op jit(solution)/shard_map/ppermute | solution.py:17
  194.8 66.0 %copy-start.2 = (bf16[128,4,1792]{2,0,1:T(8,128)(2,1)S(1)}, bf16[128,4,1792]{2,0,1:T(8,128)(2,1)}, u32[]{:S(2)}) copy-start(bf16[128,4,1792]{2,0,1:T(8,128)(2,1)} %copy-done.1) | copy-start | bytes 5505028
  256.5 83.7 %collective-permute-start.5 = (bf16[512,1792]{1,0:T(8,128)(2,1)S(1)}, bf16[512,1792]{1,0:T(8,128)(2,1)S(1)}, u32[]{:S(2)}, u32[]{:S(2)}) collective-permute-start(bf16[512,1792]{1,0:T(8,128)(2,1)S(1)} %bitcast.65), channel_id=1, source_target_pairs={{0,8},{4,12},{8,16},{12,20},{16,24},{20,28},{1,9},{5,13},{9,17},{1... | collective-permute-start | bytes 5505032 | tf_op jit(solution)/shard_map/ppermute | solution.py:17
  259.4 82.3 %collective-permute-start.6 = (bf16[512,1792]{1,0:T(8,128)(2,1)S(1)}, bf16[512,1792]{1,0:T(8,128)(2,1)S(1)}, u32[]{:S(2)}, u32[]{:S(2)}) collective-permute-start(bf16[512,1792]{1,0:T(8,128)(2,1)S(1)} %bitcast.66), channel_id=1, source_target_pairs={{0,4},{4,8},{8,12},{12,16},{16,20},{20,24},{24,28},{1,5},{5,9},{9,... | collective-permute-start | bytes 5505032 | tf_op jit(solution)/shard_map/ppermute | solution.py:17
  260.9 76.6 %copy-start.3 = (bf16[4096,1792]{1,0:T(8,128)(2,1)}, bf16[4096,1792]{1,0:T(8,128)(2,1)S(1)}, u32[]{:S(2)}) copy-start(bf16[4096,1792]{1,0:T(8,128)(2,1)S(1)} %constant_dynamic-update-slice_fusion.8) | copy-start | bytes 44040196
where the time goes:
time: 1120 us; the launch traced here: 1110 us
  matrix products  309 us (28%)
  waiting for transfers between devices  279 us (25%)
  blocking collectives  211 us (19%)
  local copies, waits for them, and re-layouts  130 us (12%)
  other arithmetic  130 us (12%)
  starting transfers between devices  30.7 us (3%)
  loops' own time  19.5 us (2%)
    ppermute x14, waiting for transfers between devices, passed_along(): return lax.ppermute(x, axis, pairs)  240 us
    all_to_all x1, blocking collectives, on_device(): lax.all_to_all(attended_group, 'head', split_axis=0, concat_axis=1, tiled...  211 us
    dot_general x90, matrix products, tile_step(): lax.dot_general(query_block, key_tile, (((1,), (1,)), ((), ())), preferre...  182 us
    dot_general x90, matrix products, tile_step(): jnp.dot(weights.astype(jnp.bfloat16), value_tile, preferred_element_type=...  128 us
    reduce_sum x90, other arithmetic, tile_step(): weight_sum = weight_sum * shrink + jnp.sum(weights, axis=1, keepdims=True)  111 us
    dynamic_slice x16, local copies, waits for them, and re-layouts, head_step(): values_head = lax.dynamic_slice_in_dim(values_all, column, head_width, 1)  46.9 us
    all_to_all x1, waiting for transfers between devices, on_device(): lax.all_to_all(value_in, 'head', split_axis=1, concat_axis=0, tiled=True)  39.2 us
    unnamed x22, local copies, waits for them, and re-layouts  22.8 us
  transfers between devices with their start and end apart: 17, of which 5 were waited for; matrix products, arithmetic and copies ran while one was open for 3% of the time, Pallas kernels for 0%

commit v1 on v0

v1 whole, which is shorter than its diff:
```python
import functools
import math

import jax
import jax.numpy as jnp
from jax import lax
from jax.experimental import pallas as pl
from jax.experimental.pallas import tpu as pltpu
from jax.sharding import PartitionSpec as P

BLOCK = 128
MIN_BAND = 16
MAX_BAND = 40
AXES = ("seq", "head")
LANES = 128
DEAD = -1e30
LOG2E = 1.4426950408889634


def turn_in_kernel(q_ref, k_ref, v_ref, out_ref):
    heads, _, width, rows = out_ref.shape
    for which, ref in enumerate((q_ref, k_ref, v_ref)):
        turned = ref[...].T
        for head in range(heads):
            out_ref[head, which] = turned[head * width : (head + 1) * width]


def turn_in(query, key, value, first, heads, width):
    rows = query.shape[0]
    step = LANES // math.gcd(width, LANES)
    start = first // step
    spec = pl.BlockSpec((rows, step * width), lambda i: (0, i + start))
    return pl.pallas_call(
        turn_in_kernel,
        grid=(heads // step,),
        in_specs=[spec] * 3,
        out_specs=pl.BlockSpec((step, 3, width, rows), lambda i: (i, 0, 0, 0)),
        out_shape=jax.ShapeDtypeStruct((heads, 3, width, rows), query.dtype),
        cost_estimate=pl.CostEstimate(
            flops=0, transcendentals=0, bytes_accessed=12 * heads * width * rows
        ),
        name="turn_in",
    )(query, key, value)


def turn_out_kernel(in_ref, out_ref):
    heads, width, rows = in_ref.shape
    out_ref[...] = in_ref[...].reshape(heads * width, rows).T


def turn_out(parts):
    heads, width, rows = parts.shape
    step = LANES // math.gcd(width, LANES)
    return pl.pallas_call(
        turn_out_kernel,
        grid=(heads // step,),
        in_specs=[pl.BlockSpec((step, width, rows), lambda i: (i, 0, 0))],
        out_specs=pl.BlockSpec((rows, step * width), lambda i: (0, i)),
        out_shape=jax.ShapeDtypeStruct((rows, heads * width), parts.dtype),
        cost_estimate=pl.CostEstimate(
            flops=0, transcendentals=0, bytes_accessed=4 * heads * width * rows
        ),
        name="turn_out",
    )(parts)


def attend_kernel(heads_total, slope_ref, band_ref, qkv_ref, out_ref, keys, values):
    blocks, _, width, rows = qkv_ref.shape
    pad = LANES - width
    tile = 2 * rows
    factor = LOG2E * width**-0.5
    slope = slope_ref[0]
    band = band_ref[0]

    row16 = lax.broadcasted_iota(jnp.int32, (pad, rows), 0)
    lane = lax.broadcasted_iota(jnp.int32, (pad, rows), 1)

    def fill(block, carry):
        at = pl.multiple_of(block * rows, rows)
        bias = (slope * (width**0.5)) * (at + lane).astype(jnp.float32)
        high = bias.astype(jnp.bfloat16).astype(jnp.float32)
        rest = bias - high
        middle = rest.astype(jnp.bfloat16).astype(jnp.float32)
        low = rest - middle
        extra = jnp.where(
            row16 == 0, high, jnp.where(row16 == 1, middle, jnp.where(row16 == 2, low, 0.0))
        ).astype(jnp.bfloat16)
        keys[pl.ds(at, rows), :] = jnp.concatenate([qkv_ref[block, 1], extra], axis=0).T
        values[:width, pl.ds(at, rows)] = qkv_ref[block, 2]
        values[width:, pl.ds(at, rows)] = jnp.ones((pad, rows), jnp.bfloat16)
        return carry

    lax.fori_loop(0, blocks, fill, 0)

    ones = jnp.ones((pad, tile), jnp.bfloat16)

    def attend_tile(index, carry):
        first = 2 * index
        query = jnp.concatenate([qkv_ref[first, 0], qkv_ref[first + 1, 0]], axis=1)
        query = jnp.concatenate([query, ones], axis=0)

        def scores(start, count):
            return jnp.dot(
                keys[pl.ds(start, count), :], query, preferred_element_type=jnp.float32
            )

        def weighed(weights, start, count):
            return jnp.dot(
                values[:, pl.ds(start, count)],
                weights.astype(jnp.bfloat16),
                preferred_element_type=jnp.float32,
            )

        def step(start, count, live, state):
            top, total = state
            score = scores(start, count)
            if live is not None:
                score = jnp.where(live(start, count), score, DEAD)
            new_top = jnp.maximum(top, jnp.max(score, axis=0, keepdims=True))
            weights = jnp.exp2(score * factor - new_top * factor)
            shrink = jnp.exp2((top - new_top) * factor)
            return new_top, total * shrink + weighed(weights, start, count)

        def live(start, count):
            key_pos = start + lax.broadcasted_iota(jnp.int32, (count, tile), 0)
            query_pos = first * rows + lax.broadcasted_iota(jnp.int32, (count, tile), 1)
            return (query_pos >= key_pos) & (query_pos // BLOCK - key_pos // BLOCK < band)

        state = (
            jnp.full((1, tile), DEAD, jnp.float32),
            jnp.zeros((LANES, tile), jnp.float32),
        )
        state = step(pl.multiple_of(first * rows, tile), tile, live, state)
        pairs = jnp.minimum(first, band - 2) // 2
        quads = pairs // 2
        edge = jnp.where(first > 2 * pairs, 1, 0)

        def quad_step(j, state):
            start = pl.multiple_of((first - 4 * (j + 1)) * rows, tile)
            return step(start, 2 * tile, None, state)

        state = lax.fori_loop(0, quads, quad_step, state)

        def pair_step(j, state):
            start = pl.multiple_of((first - 4 * quads - 2 * (j + 1)) * rows, tile)
            return step(start, tile, live, state)

        state = lax.fori_loop(0, pairs - 2 * quads + edge, pair_step, state)
        total = state[1]
        result = (total[:width] / total[width : width + 1]).astype(jnp.bfloat16)
        out_ref[first] = result[:, :rows]
        out_ref[first + 1] = result[:, rows:]
        return carry

    lax.fori_loop(0, blocks // 2, attend_tile, 0)


def attend(qkv, slope, band, heads_total):
    blocks, _, width, rows = qkv.shape
    pairs = blocks * (blocks + 1) // 2
    return pl.pallas_call(
        functools.partial(attend_kernel, heads_total),
        in_specs=[
            pl.BlockSpec(memory_space=pltpu.SMEM),
            pl.BlockSpec(memory_space=pltpu.SMEM),
            pl.BlockSpec(memory_space=pltpu.VMEM),
        ],
        out_specs=pl.BlockSpec(memory_space=pltpu.VMEM),
        out_shape=jax.ShapeDtypeStruct((blocks, width, rows), jnp.bfloat16),
        scratch_shapes=[
            pltpu.VMEM((blocks * rows, LANES), jnp.bfloat16),
            pltpu.VMEM((LANES, blocks * rows), jnp.bfloat16),
        ],
        compiler_params=pltpu.CompilerParams(vmem_limit_bytes=40 * 2**20),
        cost_estimate=pl.CostEstimate(
            flops=4 * pairs * rows * rows * LANES,
            transcendentals=pairs * rows * rows,
            bytes_accessed=8 * blocks * width * rows,
        ),
        name="attend",
    )(slope, band, qkv)


def on_device(query, key, value, exponent):
    rows, width_total = query.shape
    heads = exponent.shape[0]
    width = width_total // heads
    devices = lax.axis_size("seq") * lax.axis_size("head")
    me = lax.axis_index("seq") * lax.axis_size("head") + lax.axis_index("head")
    share = max(1, devices // heads)
    owners = devices // share
    rounds = heads // owners

    band = MIN_BAND + (exponent - 1) * (MAX_BAND - MIN_BAND) // (heads - 1)
    slope = jnp.exp2(-12.0 * exponent.astype(jnp.float32) / heads)

    outs = []
    for part in range(rounds):
        sent = turn_in(query, key, value, part * owners, owners, width)
        if share > 1:
            sent = jnp.repeat(sent, share, axis=0)
        qkv = lax.all_to_all(sent, AXES, 0, 0, tiled=True)
        head = part * owners + me // share
        mine = lax.dynamic_slice_in_dim(slope, head, 1), lax.dynamic_slice_in_dim(band, head, 1)
        result = attend(qkv, *mine, heads)
        back = lax.all_to_all(result, AXES, 0, 0, tiled=True)
        if share > 1:
            back = back.reshape(owners, share, width, rows)[:, 0]
        outs.append(turn_out(back))
    return jnp.concatenate(outs, axis=1)


def solution(mesh):
    spec = P(AXES, None)
    return jax.shard_map(
        on_device,
        mesh=mesh,
        in_specs=(spec, spec, spec, P()),
        out_specs=spec,
        check_vma=False,
    )
```

time: 1120 us -> 230 us (0.21)
  matrix products: 309 us -> 0 us
  blocking collectives: 211 us -> 0 us
  waiting for transfers between devices: 279 us -> 89.1 us
  other arithmetic: 130 us -> 2.86 us
  local copies, waits for them, and re-layouts: 130 us -> 7.44 us
  Pallas kernels: 0 us -> 106 us
  loops' own time: 19.5 us -> 0 us
    dot_general x180 -> x0, matrix products: 309 us -> none  [the longest x90 182 us: tile_step(): lax.dot_general(query_block, key_tile, (((1,), (1,)), ((), ())), preferre...]
    ppermute x14 -> x0, waiting for transfers between devices: 240 us -> none  [passed_along(): return lax.ppermute(x, axis, pairs)]
    all_to_all x1 -> x0, blocking collectives: 211 us -> none  [on_device(): lax.all_to_all(attended_group, 'head', split_axis=0, concat_axis=1, tiled...]
    reduce_sum x90 -> x0, other arithmetic: 111 us -> none  [tile_step(): weight_sum = weight_sum * shrink + jnp.sum(weights, axis=1, keepdims=True)]
    pallas_call x0 -> x6, Pallas kernels: none -> 106 us  [the longest x2 90.2 us: attend(): pl.pallas_call(functools.partial(attend_kernel, heads_total), in_specs=[p...]
    dynamic_slice x64 -> x2, local copies, waits for them, and re-layouts: 84.9 us -> 1.32 us  [the longest x1 0.67 us: on_device(): lax.dynamic_slice_in_dim(slope, head, 1)]
    all_to_all x3 -> x4, waiting for transfers between devices: 39.2 us -> 89.1 us  [the longest x2 70.2 us: on_device(): qkv = lax.all_to_all(sent, AXES, 0, 0, tiled=True)]
    another operation x17 -> x0, loops' own time: 19.5 us -> none  [the longest x1 12.2 us: on_device(): lax.fori_loop(0, local_heads, head_step, jnp.zeros((group_rows, local_wid...]
  transfers between devices with their start and end apart: 17 -> 4, of which waited for: 5 -> 3; matrix products, arithmetic and copies ran while one was open for 3% -> 1% of each run, Pallas kernels for 0% -> 43%
where the time goes in v1:
time: 230 us; the launch traced here: 227 us
  Pallas kernels  106 us (46%)
  waiting for transfers between devices  89.1 us (39%)
  starting transfers between devices  21.5 us (9%)
  local copies, waits for them, and re-layouts  7.44 us (3%)
  other arithmetic  2.86 us (1%)
    pallas_call x2, Pallas kernels, attend(): pl.pallas_call(functools.partial(attend_kernel, heads_total), in_specs=[p...  90.2 us
    all_to_all x2, waiting for transfers between devices, on_device(): qkv = lax.all_to_all(sent, AXES, 0, 0, tiled=True)  70.2 us
    all_to_all x2, waiting for transfers between devices, on_device(): back = lax.all_to_all(result, AXES, 0, 0, tiled=True)  18.9 us
    all_to_all x2, starting transfers between devices, on_device(): back = lax.all_to_all(result, AXES, 0, 0, tiled=True)  10.8 us
    all_to_all x2, starting transfers between devices, on_device(): qkv = lax.all_to_all(sent, AXES, 0, 0, tiled=True)  10.7 us
    pallas_call x2, Pallas kernels, turn_in(): pl.pallas_call(turn_in_kernel, grid=(heads // step,), in_specs=[spec] * 3...  9 us
    pallas_call x2, Pallas kernels, turn_out(): pl.pallas_call(turn_out_kernel, grid=(heads // step,), in_specs=[pl.Block...  7.14 us
    unnamed x12, local copies, waits for them, and re-layouts  6.12 us
  transfers between devices with their start and end apart: 4, of which 3 were waited for; matrix products, arithmetic and copies ran while one was open for 1% of the time, Pallas kernels for 43%

profile of v1, /device:TPU:7, one launch (start us, length us, event | category | flops | bytes accessed | tf_op | source)
XLA Modules:
  0.0 227.3 jit_solution(8776606066406539815)
XLA Ops:
  0.0 4.5 %turn_in.3 = bf16[32,3,112,128]{3,2,1,0:T(8,128)(2,1)} custom-call(bf16[128,7168]{1,0:T(8,128)(2,1)} %q_ref.3, bf16[128,7168]{1,0:T(8,128)(2,1)} %k_ref.3, bf16[128,7168]{1,0:T(8,128)(2,1)} %v_ref.3), custom_call_target="tpu_custom_call" | custom-call | bytes 5505024 | tf_op jit(solution)/shard_map/turn_in/pallas_call | solution.py:33
  4.5 6.4 %all-to-all-start.2 = ((bf16[32,3,112,128]{3,2,1,0:T(8,128)(2,1)}), bf16[32,3,112,128]{3,2,1,0:T(8,128)(2,1)S(1)}, u32[]{:S(2)}, u32[]{:S(2)}) async-start(bf16[32,3,112,128]{3,2,1,0:T(8,128)(2,1)} %turn_in.3), calls=%async_computation.2 | async-start | bytes 5505024 | tf_op jit(solution)/shard_map/all_to_all | solution.py:202
  10.9 4.5 %turn_in.2 = bf16[32,3,112,128]{3,2,1,0:T(8,128)(2,1)} custom-call(bf16[128,7168]{1,0:T(8,128)(2,1)} %q_ref.3, bf16[128,7168]{1,0:T(8,128)(2,1)} %k_ref.3, bf16[128,7168]{1,0:T(8,128)(2,1)} %v_ref.3), custom_call_target="tpu_custom_call" | custom-call | bytes 5505024 | tf_op jit(solution)/shard_map/turn_in/pallas_call | solution.py:33
  15.4 57.6 %all-to-all-done.2.qkv_ref = bf16[32,3,112,128]{3,2,1,0:T(8,128)(2,1)S(1)} async-done(((bf16[32,3,112,128]{3,2,1,0:T(8,128)(2,1)}), bf16[32,3,112,128]{3,2,1,0:T(8,128)(2,1)S(1)}, u32[]{:S(2)}, u32[]{:S(2)}) %all-to-all-start.2) | async-done | bytes 2752544 | tf_op jit(solution)/shard_map/all_to_all | solution.py:202
  73.0 1.6 copy-done
  74.6 4.3 %all-to-all-start = ((bf16[32,3,112,128]{3,2,1,0:T(8,128)(2,1)}), bf16[32,3,112,128]{3,2,1,0:T(8,128)(2,1)S(1)}, u32[]{:S(2)}, u32[]{:S(2)}) async-start(bf16[32,3,112,128]{3,2,1,0:T(8,128)(2,1)} %turn_in.2), calls=%async_computation | async-start | bytes 5505024 | tf_op jit(solution)/shard_map/all_to_all | solution.py:202
  78.9 0.0 copy-done.5
  78.9 0.7 fusion.2
  79.6 0.6 fusion.1
  80.2 1.8 copy-done.1
  82.0 45.4 %attend.3 = bf16[32,112,128]{2,1,0:T(8,128)(2,1)S(1)} custom-call(f32[1]{0:T(128)} %get-tuple-element.8.slope_ref, s32[1]{0:T(128)} %get-tuple-element.6.band_ref, bf16[32,3,112,128]{3,2,1,0:T(8,128)(2,1)S(1)} %copy-done.1), custom_call_target="tpu_custom_call" | custom-call | flops 4429185024 | bytes 3670016 | tf_op jit(solution)/shard_map/attend/pallas_call | solution.py:161
  127.5 0.0 copy-start.2
  127.5 0.9 copy-done.2
  128.4 12.6 %all-to-all-done.qkv_ref = bf16[32,3,112,128]{3,2,1,0:T(8,128)(2,1)S(1)} async-done(((bf16[32,3,112,128]{3,2,1,0:T(8,128)(2,1)}), bf16[32,3,112,128]{3,2,1,0:T(8,128)(2,1)S(1)}, u32[]{:S(2)}, u32[]{:S(2)}) %all-to-all-start) | async-done | bytes 2752544 | tf_op jit(solution)/shard_map/all_to_all | solution.py:202
  141.0 4.3 %all-to-all-start.3 = ((bf16[32,112,128]{2,1,0:T(8,128)(2,1)}), bf16[32,112,128]{2,1,0:T(8,128)(2,1)}, u32[]{:S(2)}, u32[]{:S(2)}) async-start(bf16[32,112,128]{2,1,0:T(8,128)(2,1)} %copy-done.2), calls=%async_computation.3 | async-start | bytes 1835008 | tf_op jit(solution)/shard_map/all_to_all | solution.py:206
  145.3 44.8 %attend.2 = bf16[32,112,128]{2,1,0:T(8,128)(2,1)S(1)} custom-call(f32[1]{0:T(128)} %get-tuple-element.7.slope_ref, s32[1]{0:T(128)} %get-tuple-element.5.band_ref, bf16[32,3,112,128]{3,2,1,0:T(8,128)(2,1)S(1)} %all-to-all-done.qkv_ref), custom_call_target="tpu_custom_call" | custom-call | flops 4429185024 | bytes 3670016 | tf_op jit(solution)/shard_map/attend/pallas_call | solution.py:161
  190.1 0.9 copy-done.3
  191.0 0.0 all-to-all-done.3.in_ref
  191.0 6.5 %all-to-all-start.1 = ((bf16[32,112,128]{2,1,0:T(8,128)(2,1)}), bf16[32,112,128]{2,1,0:T(8,128)(2,1)S(1)}, u32[]{:S(2)}, u32[]{:S(2)}) async-start(bf16[32,112,128]{2,1,0:T(8,128)(2,1)} %copy-done.3), calls=%async_computation.1 | async-start | bytes 1835008 | tf_op jit(solution)/shard_map/all_to_all | solution.py:206
  197.5 3.6 %turn_out.3 = bf16[128,3584]{1,0:T(8,128)(2,1)} custom-call(bf16[32,112,128]{2,1,0:T(8,128)(2,1)} %all-to-all-done.3.in_ref), custom_call_target="tpu_custom_call" | custom-call | bytes 1835008 | tf_op jit(solution)/shard_map/turn_out/pallas_call | solution.py:54
  201.1 18.9 %all-to-all-done.1.in_ref = bf16[32,112,128]{2,1,0:T(8,128)(2,1)S(1)} async-done(((bf16[32,112,128]{2,1,0:T(8,128)(2,1)}), bf16[32,112,128]{2,1,0:T(8,128)(2,1)S(1)}, u32[]{:S(2)}, u32[]{:S(2)}) %all-to-all-start.1) | async-done | bytes 917536 | tf_op jit(solution)/shard_map/all_to_all | solution.py:206
  220.0 0.9 copy-done.4
  220.9 3.6 %turn_out.2 = bf16[128,3584]{1,0:T(8,128)(2,1)} custom-call(bf16[32,112,128]{2,1,0:T(8,128)(2,1)} %copy-done.4), custom_call_target="tpu_custom_call" | custom-call | bytes 1835008 | tf_op jit(solution)/shard_map/turn_out/pallas_call | solution.py:54
  224.5 2.8 %pad_maximum_fusion = bf16[128,7168]{1,0:T(8,128)(2,1)} fusion(bf16[128,3584]{1,0:T(8,128)(2,1)} %turn_out.3, bf16[128,3584]{1,0:T(8,128)(2,1)} %turn_out.2), kind=kLoop, calls=%fused_computation | loop fusion | flops 3670016 | bytes 3670016 | tf_op jit(solution)/shard_map/concatenate | solution.py:210
  (7 shorter events, 0.0 us)
Async XLA Ops:
  4.5 68.5 %all-to-all-start.2 = ((bf16[32,3,112,128]{3,2,1,0:T(8,128)(2,1)}), bf16[32,3,112,128]{3,2,1,0:T(8,128)(2,1)S(1)}, u32[]{:S(2)}, u32[]{:S(2)}) async-start(bf16[32,3,112,128]{3,2,1,0:T(8,128)(2,1)} %turn_in.3), calls=%async_computation.2 | async-start | bytes 5505024 | tf_op jit(solution)/shard_map/all_to_all | solution.py:202
  15.4 63.5 %copy-start.5 = (s32[64]{0:T(128)S(1)}, s32[64]{0:T(128)}, u32[]{:S(2)}) copy-start(s32[64]{0:T(128)} %param.7) | copy-start | bytes 772
  73.0 1.6 copy-start
  74.6 66.4 %all-to-all-start = ((bf16[32,3,112,128]{3,2,1,0:T(8,128)(2,1)}), bf16[32,3,112,128]{3,2,1,0:T(8,128)(2,1)S(1)}, u32[]{:S(2)}, u32[]{:S(2)}) async-start(bf16[32,3,112,128]{3,2,1,0:T(8,128)(2,1)} %turn_in.2), calls=%async_computation | async-start | bytes 5505024 | tf_op jit(solution)/shard_map/all_to_all | solution.py:202
  80.2 1.8 copy-start.1
  127.5 0.9 copy-start.2
  141.0 50.1 %all-to-all-start.3 = ((bf16[32,112,128]{2,1,0:T(8,128)(2,1)}), bf16[32,112,128]{2,1,0:T(8,128)(2,1)}, u32[]{:S(2)}, u32[]{:S(2)}) async-start(bf16[32,112,128]{2,1,0:T(8,128)(2,1)} %copy-done.2), calls=%async_computation.3 | async-start | bytes 1835008 | tf_op jit(solution)/shard_map/all_to_all | solution.py:206
  190.1 0.9 copy-start.3
  191.0 29.0 %all-to-all-start.1 = ((bf16[32,112,128]{2,1,0:T(8,128)(2,1)}), bf16[32,112,128]{2,1,0:T(8,128)(2,1)S(1)}, u32[]{:S(2)}, u32[]{:S(2)}) async-start(bf16[32,112,128]{2,1,0:T(8,128)(2,1)} %copy-done.3), calls=%async_computation.1 | async-start | bytes 1835008 | tf_op jit(solution)/shard_map/all_to_all | solution.py:206
  220.0 0.9 copy-start.4

commit v2 on v1

v2 whole, which is shorter than its diff:
```python
import functools
import math

import jax
import jax.numpy as jnp
from jax import lax
from jax.experimental import pallas as pl
from jax.experimental.pallas import tpu as pltpu
from jax.sharding import PartitionSpec as P

BLOCK = 128
MIN_BAND = 16
MAX_BAND = 40
AXES = ("seq", "head")
LANES = 128
DEAD = -1e30
LOG2E = 1.4426950408889634
PIECE = 256
SPAN = 100.0


def turn_in_kernel(q_ref, k_ref, v_ref, out_ref):
    heads, _, width, rows = out_ref.shape
    for which, ref in enumerate((q_ref, k_ref, v_ref)):
        turned = ref[...].T
        for head in range(heads):
            out_ref[head, which] = turned[head * width : (head + 1) * width]


def turn_in(query, key, value, first, heads, width):
    rows = query.shape[0]
    step = LANES // math.gcd(width, LANES)
    start = first // step
    spec = pl.BlockSpec((rows, step * width), lambda i: (0, i + start))
    return pl.pallas_call(
        turn_in_kernel,
        grid=(heads // step,),
        in_specs=[spec] * 3,
        out_specs=pl.BlockSpec((step, 3, width, rows), lambda i: (i, 0, 0, 0)),
        out_shape=jax.ShapeDtypeStruct((heads, 3, width, rows), query.dtype),
        cost_estimate=pl.CostEstimate(
            flops=0, transcendentals=0, bytes_accessed=12 * heads * width * rows
        ),
        name="turn_in",
    )(query, key, value)


def turn_out_kernel(in_ref, *refs):
    heads, width, rows = in_ref.shape
    refs[-1][...] = in_ref[...].reshape(heads * width, rows).T


def turn_out(parts, first, so_far, heads_total):
    heads, width, rows = parts.shape
    step = LANES // math.gcd(width, LANES)
    start = first // step
    given = () if so_far is None else (so_far,)
    return pl.pallas_call(
        turn_out_kernel,
        grid=(heads // step,),
        in_specs=[pl.BlockSpec((step, width, rows), lambda i: (i, 0, 0))]
        + [pl.BlockSpec(memory_space=pl.ANY)] * len(given),
        out_specs=pl.BlockSpec((rows, step * width), lambda i: (0, i + start)),
        out_shape=jax.ShapeDtypeStruct((rows, heads_total * width), parts.dtype),
        input_output_aliases={1: 0} if given else {},
        cost_estimate=pl.CostEstimate(
            flops=0, transcendentals=0, bytes_accessed=4 * heads * width * rows
        ),
        name="turn_out",
    )(parts, *given)


def attend_kernel(sub, slope_ref, band_ref, qkv_ref, out_ref, keys, values):
    blocks, _, width, rows = qkv_ref.shape
    pad = LANES - width
    half = 2 * rows
    per = 2 * sub
    factor = LOG2E * width**-0.5
    slope = slope_ref[0]
    band = band_ref[0]

    row = lax.broadcasted_iota(jnp.int32, (pad, rows), 0)
    lane = lax.broadcasted_iota(jnp.int32, (pad, rows), 1)

    def fill(block, carry):
        at = pl.multiple_of(block * rows, rows)
        bias = (slope * width**0.5) * (at + lane).astype(jnp.float32)
        high = bias.astype(jnp.bfloat16).astype(jnp.float32)
        rest = bias - high
        middle = rest.astype(jnp.bfloat16).astype(jnp.float32)
        low = rest - middle
        extra = jnp.where(
            row == 0, high, jnp.where(row == 1, middle, jnp.where(row == 2, low, 0.0))
        ).astype(jnp.bfloat16)
        keys[pl.ds(at, rows), :] = jnp.concatenate([qkv_ref[block, 1], extra], axis=0).T
        values[:width, pl.ds(at, rows)] = qkv_ref[block, 2]
        values[width:, pl.ds(at, rows)] = jnp.ones((pad, rows), jnp.bfloat16)
        return carry

    lax.fori_loop(0, blocks, fill, 0, unroll=4)
    ones = jnp.ones((pad, half), jnp.bfloat16)

    def attend_tile(index, carry):
        first = per * index

        def query_of(s):
            pair = [qkv_ref[first + 2 * s, 0], qkv_ref[first + 2 * s + 1, 0]]
            return jnp.concatenate([jnp.concatenate(pair, axis=1), ones], axis=0)

        def live(start, count, s):
            key_pos = start + lax.broadcasted_iota(jnp.int32, (count, half), 0)
            query_pos = (first + 2 * s) * rows + lax.broadcasted_iota(jnp.int32, (count, half), 1)
            return (query_pos >= key_pos) & (query_pos // BLOCK - key_pos // BLOCK < band)

        def scored(start, count, s, masked, query):
            score = jnp.dot(keys[pl.ds(start, count), :], query, preferred_element_type=jnp.float32)
            return jnp.where(live(start, count, s), score, DEAD) if masked else score

        def weighed(start, count, weights):
            return jnp.dot(
                values[:, pl.ds(start, count)],
                weights.astype(jnp.bfloat16),
                preferred_element_type=jnp.float32,
            )

        def slow_step(start, count, s, masked, query, state):
            top, total = state
            score = scored(start, count, s, masked, query)
            new_top = jnp.maximum(top, jnp.max(score, axis=0, keepdims=True))
            weights = jnp.exp2(score * factor - new_top * factor)
            shrink = jnp.exp2((top - new_top) * factor)
            return new_top, total * shrink + weighed(start, count, weights)

        def fast_step(start, count, s, masked, query, state):
            top, total, high = state
            pieces = []
            for at in range(0, count, PIECE):
                score = scored(start + at, PIECE, s, masked, query)
                pieces.append(jnp.exp2(score * factor - top * factor).astype(jnp.bfloat16))
                high = jnp.maximum(high, jnp.max(score.reshape(PIECE // 8, 8, half), axis=0))
            return top, total + weighed(start, count, jnp.concatenate(pieces, axis=0)), high

        whole = jnp.minimum(first, band - per) // per
        needed = jnp.minimum(first, band - 1)
        rest = (needed - per * whole + per - 1) // per

        def sweep(step, queries, states):
            def steps(masked):
                def body(j, states):
                    start = pl.multiple_of((first - per * (j + 1)) * rows, half)
                    return [
                        step(start, per * rows, s, masked, queries[s], states[s])
                        for s in range(sub)
                    ]

                return body

            states = lax.fori_loop(0, whole, steps(False), states)
            return lax.fori_loop(whole, whole + rest, steps(True), states)

        def finish(s, total):
            result = (total[:width] / total[width : width + 1]).astype(jnp.bfloat16)
            out_ref[first + 2 * s] = result[:, :rows]
            out_ref[first + 2 * s + 1] = result[:, rows:]

        queries = [query_of(s) for s in range(sub)]
        states = []
        for s in range(sub):
            start = pl.multiple_of((first + 2 * s) * rows, half)
            score = scored(start, half, s, True, queries[s])
            top = jnp.max(score, axis=0, keepdims=True)
            total = weighed(start, half, jnp.exp2(score * factor - top * factor))
            state = (top, total, jnp.full((8, half), DEAD, jnp.float32))
            if s:
                start = pl.multiple_of(first * rows, half)
                state = fast_step(start, half * s, s, False, queries[s], state)
            states.append(state)
        states = sweep(fast_step, queries, states)
        worst = jnp.float32(DEAD)
        for s in range(sub):
            top, total, high = states[s]
            finish(s, total)
            worst = jnp.maximum(worst, jnp.max(high - top))

        @pl.when(worst * factor > SPAN)
        def _():
            queries = [query_of(s) for s in range(sub)]
            states = []
            for s in range(sub):
                state = (
                    jnp.full((1, half), DEAD, jnp.float32),
                    jnp.zeros((LANES, half), jnp.float32),
                )
                start = pl.multiple_of(first * rows, half)
                states.append(slow_step(start, half * (s + 1), s, True, queries[s], state))
            states = sweep(slow_step, queries, states)
            for s in range(sub):
                finish(s, states[s][1])

        return carry

    lax.fori_loop(0, blocks // per, attend_tile, 0)


def attend(qkv, slope, band, heads_total):
    blocks, _, width, rows = qkv.shape
    pairs = blocks * (blocks + 1) // 2
    sub = math.gcd(blocks, 8) // 2
    return pl.pallas_call(
        functools.partial(attend_kernel, sub),
        in_specs=[
            pl.BlockSpec(memory_space=pltpu.SMEM),
            pl.BlockSpec(memory_space=pltpu.SMEM),
            pl.BlockSpec(memory_space=pltpu.VMEM),
        ],
        out_specs=pl.BlockSpec(memory_space=pltpu.VMEM),
        out_shape=jax.ShapeDtypeStruct((blocks, width, rows), jnp.bfloat16),
        scratch_shapes=[
            pltpu.VMEM((blocks * rows, LANES), jnp.bfloat16),
            pltpu.VMEM((LANES, blocks * rows), jnp.bfloat16),
        ],
        compiler_params=pltpu.CompilerParams(vmem_limit_bytes=32 * 2**20),
        cost_estimate=pl.CostEstimate(
            flops=4 * pairs * rows * rows * LANES,
            transcendentals=pairs * rows * rows,
            bytes_accessed=8 * blocks * width * rows,
        ),
        name="attend",
    )(slope, band, qkv)


def on_device(query, key, value, exponent):
    rows, width_total = query.shape
    heads = exponent.shape[0]
    width = width_total // heads
    devices = lax.axis_size("seq") * lax.axis_size("head")
    me = lax.axis_index("seq") * lax.axis_size("head") + lax.axis_index("head")
    share = max(1, devices // heads)
    owners = devices // share
    rounds = heads // owners

    band = MIN_BAND + (exponent - 1) * (MAX_BAND - MIN_BAND) // (heads - 1)
    slope = jnp.exp2(-12.0 * exponent.astype(jnp.float32) / heads)

    out = None
    for part in range(rounds):
        sent = turn_in(query, key, value, part * owners, owners, width)
        if share > 1:
            sent = jnp.repeat(sent, share, axis=0)
        qkv = lax.all_to_all(sent, AXES, 0, 0, tiled=True)
        head = part * owners + me // share
        mine = lax.dynamic_slice_in_dim(slope, head, 1), lax.dynamic_slice_in_dim(band, head, 1)
        result = attend(qkv, *mine, heads)
        back = lax.all_to_all(result, AXES, 0, 0, tiled=True)
        if share > 1:
            back = back.reshape(owners, share, width, rows)[:, 0]
        out = turn_out(back, part * owners, out, heads)
    return out


def solution(mesh):
    spec = P(AXES, None)
    return jax.shard_map(
        on_device,
        mesh=mesh,
        in_specs=(spec, spec, spec, P()),
        out_specs=spec,
        check_vma=False,
    )
```

time: 230 us -> 202 us (0.88)
  Pallas kernels: 106 us -> 51.4 us
  waiting for transfers between devices: 89.1 us -> 121 us
  other arithmetic: 2.86 us -> 0.02 us
    pallas_call x2, Pallas kernels: 90.2 us -> 35.3 us  [attend(): pl.pallas_call(functools.partial(attend_kernel, sub), in_specs=[pl.BlockS...]
    all_to_all x2, waiting for transfers between devices: 70.2 us -> 97.6 us  [on_device(): qkv = lax.all_to_all(sent, AXES, 0, 0, tiled=True)]
    all_to_all x2, waiting for transfers between devices: 18.9 us -> 23.2 us  [on_device(): back = lax.all_to_all(result, AXES, 0, 0, tiled=True)]
    concatenate x1 -> x0, other arithmetic: 2.84 us -> none  [on_device(): return jnp.concatenate(outs, axis=1)]
  transfers between devices with their start and end apart: 4 -> 4, of which waited for: 3 -> 4; matrix products, arithmetic and copies ran while one was open for 1% -> 1% of each run, Pallas kernels for 43% -> 22%
where the time goes in v2:
time: 202 us; the launch traced here: 199 us
  waiting for transfers between devices  121 us (60%)
  Pallas kernels  51.4 us (25%)
  starting transfers between devices  19.3 us (10%)
  local copies, waits for them, and re-layouts  7.5 us (4%)
    all_to_all x2, waiting for transfers between devices, on_device(): qkv = lax.all_to_all(sent, AXES, 0, 0, tiled=True)  97.6 us
    pallas_call x2, Pallas kernels, attend(): pl.pallas_call(functools.partial(attend_kernel, sub), in_specs=[pl.BlockS...  35.3 us
    all_to_all x2, waiting for transfers between devices, on_device(): back = lax.all_to_all(result, AXES, 0, 0, tiled=True)  23.2 us
    all_to_all x2, starting transfers between devices, on_device(): qkv = lax.all_to_all(sent, AXES, 0, 0, tiled=True)  10.7 us
    pallas_call x2, Pallas kernels, turn_in(): pl.pallas_call(turn_in_kernel, grid=(heads // step,), in_specs=[spec] * 3...  9 us
    all_to_all x2, starting transfers between devices, on_device(): back = lax.all_to_all(result, AXES, 0, 0, tiled=True)  8.6 us
    pallas_call x2, Pallas kernels, turn_out(): pl.pallas_call(turn_out_kernel, grid=(heads // step,), in_specs=[pl.Block...  7.05 us
    unnamed x12, local copies, waits for them, and re-layouts  6.18 us
  transfers between devices with their start and end apart: 4, of which 4 were waited for; matrix products, arithmetic and copies ran while one was open for 1% of the time, Pallas kernels for 22%

profile of v2, /device:TPU:7, one launch (start us, length us, event | category | flops | bytes accessed | tf_op | source)
XLA Modules:
  0.0 199.1 jit_solution(13351992213816389755)
XLA Ops:
  0.0 4.5 %turn_in.3 = bf16[32,3,112,128]{3,2,1,0:T(8,128)(2,1)} custom-call(bf16[128,7168]{1,0:T(8,128)(2,1)} %q_ref.3, bf16[128,7168]{1,0:T(8,128)(2,1)} %k_ref.3, bf16[128,7168]{1,0:T(8,128)(2,1)} %v_ref.3), custom_call_target="tpu_custom_call" | custom-call | bytes 5505024 | tf_op jit(solution)/shard_map/turn_in/pallas_call | solution.py:35
  4.5 6.4 %all-to-all-start.2 = ((bf16[32,3,112,128]{3,2,1,0:T(8,128)(2,1)}), bf16[32,3,112,128]{3,2,1,0:T(8,128)(2,1)S(1)}, u32[]{:S(2)}, u32[]{:S(2)}) async-start(bf16[32,3,112,128]{3,2,1,0:T(8,128)(2,1)} %turn_in.3), calls=%async_computation.2 | async-start | bytes 5505024 | tf_op jit(solution)/shard_map/all_to_all | solution.py:250
  10.9 4.5 %turn_in.2 = bf16[32,3,112,128]{3,2,1,0:T(8,128)(2,1)} custom-call(bf16[128,7168]{1,0:T(8,128)(2,1)} %q_ref.3, bf16[128,7168]{1,0:T(8,128)(2,1)} %k_ref.3, bf16[128,7168]{1,0:T(8,128)(2,1)} %v_ref.3), custom_call_target="tpu_custom_call" | custom-call | bytes 5505024 | tf_op jit(solution)/shard_map/turn_in/pallas_call | solution.py:35
  15.4 57.6 %all-to-all-done.2.qkv_ref = bf16[32,3,112,128]{3,2,1,0:T(8,128)(2,1)S(1)} async-done(((bf16[32,3,112,128]{3,2,1,0:T(8,128)(2,1)}), bf16[32,3,112,128]{3,2,1,0:T(8,128)(2,1)S(1)}, u32[]{:S(2)}, u32[]{:S(2)}) %all-to-all-start.2) | async-done | bytes 2752544 | tf_op jit(solution)/shard_map/all_to_all | solution.py:250
  73.0 1.6 copy-done
  74.6 4.3 %all-to-all-start = ((bf16[32,3,112,128]{3,2,1,0:T(8,128)(2,1)}), bf16[32,3,112,128]{3,2,1,0:T(8,128)(2,1)S(1)}, u32[]{:S(2)}, u32[]{:S(2)}) async-start(bf16[32,3,112,128]{3,2,1,0:T(8,128)(2,1)} %turn_in.2), calls=%async_computation | async-start | bytes 5505024 | tf_op jit(solution)/shard_map/all_to_all | solution.py:250
  78.9 0.0 copy-done.5
  78.9 0.7 fusion.2
  79.6 0.6 fusion.1
  80.2 1.8 copy-done.1
  82.0 18.0 %attend.3 = bf16[32,112,128]{2,1,0:T(8,128)(2,1)S(1)} custom-call(f32[1]{0:T(128)} %get-tuple-element.7.slope_ref, s32[1]{0:T(128)} %get-tuple-element.5.band_ref, bf16[32,3,112,128]{3,2,1,0:T(8,128)(2,1)S(1)} %copy-done.1), custom_call_target="tpu_custom_call" | custom-call | flops 4429185024 | bytes 3670016 | tf_op jit(solution)/shard_map/attend/pallas_call | solution.py:209
  100.0 0.0 copy-start.2
  100.1 0.9 copy-done.2
  101.0 40.0 %all-to-all-done.qkv_ref = bf16[32,3,112,128]{3,2,1,0:T(8,128)(2,1)S(1)} async-done(((bf16[32,3,112,128]{3,2,1,0:T(8,128)(2,1)}), bf16[32,3,112,128]{3,2,1,0:T(8,128)(2,1)S(1)}, u32[]{:S(2)}, u32[]{:S(2)}) %all-to-all-start) | async-done | bytes 2752544 | tf_op jit(solution)/shard_map/all_to_all | solution.py:250
  141.0 4.3 %all-to-all-start.3 = ((bf16[32,112,128]{2,1,0:T(8,128)(2,1)}), bf16[32,112,128]{2,1,0:T(8,128)(2,1)}, u32[]{:S(2)}, u32[]{:S(2)}) async-start(bf16[32,112,128]{2,1,0:T(8,128)(2,1)} %copy-done.2), calls=%async_computation.3 | async-start | bytes 1835008 | tf_op jit(solution)/shard_map/all_to_all | solution.py:254
  145.3 17.3 %attend.2 = bf16[32,112,128]{2,1,0:T(8,128)(2,1)S(1)} custom-call(f32[1]{0:T(128)} %get-tuple-element.8.slope_ref, s32[1]{0:T(128)} %get-tuple-element.6.band_ref, bf16[32,3,112,128]{3,2,1,0:T(8,128)(2,1)S(1)} %all-to-all-done.qkv_ref), custom_call_target="tpu_custom_call" | custom-call | flops 4429185024 | bytes 3670016 | tf_op jit(solution)/shard_map/attend/pallas_call | solution.py:209
  162.6 0.0 copy-start.3
  162.6 1.0 copy-done.3
  163.6 4.2 %all-to-all-done.3.in_ref = bf16[32,112,128]{2,1,0:T(8,128)(2,1)} async-done(((bf16[32,112,128]{2,1,0:T(8,128)(2,1)}), bf16[32,112,128]{2,1,0:T(8,128)(2,1)}, u32[]{:S(2)}, u32[]{:S(2)}) %all-to-all-start.3) | async-done | bytes 917536 | tf_op jit(solution)/shard_map/all_to_all | solution.py:254
  167.9 4.3 %all-to-all-start.1 = ((bf16[32,112,128]{2,1,0:T(8,128)(2,1)}), bf16[32,112,128]{2,1,0:T(8,128)(2,1)S(1)}, u32[]{:S(2)}, u32[]{:S(2)}) async-start(bf16[32,112,128]{2,1,0:T(8,128)(2,1)} %copy-done.3), calls=%async_computation.1 | async-start | bytes 1835008 | tf_op jit(solution)/shard_map/all_to_all | solution.py:254
  172.1 3.5 %turn_out.2.refs_0_ = bf16[128,7168]{1,0:T(8,128)(2,1)} custom-call(bf16[32,112,128]{2,1,0:T(8,128)(2,1)} %all-to-all-done.3.in_ref), custom_call_target="tpu_custom_call" | custom-call | bytes 1835008 | tf_op jit(solution)/shard_map/turn_out/pallas_call | solution.py:58
  175.7 19.0 %all-to-all-done.1.in_ref = bf16[32,112,128]{2,1,0:T(8,128)(2,1)S(1)} async-done(((bf16[32,112,128]{2,1,0:T(8,128)(2,1)}), bf16[32,112,128]{2,1,0:T(8,128)(2,1)S(1)}, u32[]{:S(2)}, u32[]{:S(2)}) %all-to-all-start.1) | async-done | bytes 917536 | tf_op jit(solution)/shard_map/all_to_all | solution.py:254
  194.6 0.9 copy-done.4
  195.5 3.5 %turn_out.3 = bf16[128,7168]{1,0:T(8,128)(2,1)} custom-call(bf16[32,112,128]{2,1,0:T(8,128)(2,1)} %copy-done.4, bf16[128,7168]{1,0:T(8,128)(2,1)} %turn_out.2.refs_0_), custom_call_target="tpu_custom_call", output_to_operand_aliasing={{}: (1, {})} | custom-call | bytes 1835008 | tf_op jit(solution)/shard_map/turn_out/pallas_call | solution.py:58
  (6 shorter events, 0.0 us)
Async XLA Ops:
  4.5 68.5 %all-to-all-start.2 = ((bf16[32,3,112,128]{3,2,1,0:T(8,128)(2,1)}), bf16[32,3,112,128]{3,2,1,0:T(8,128)(2,1)S(1)}, u32[]{:S(2)}, u32[]{:S(2)}) async-start(bf16[32,3,112,128]{3,2,1,0:T(8,128)(2,1)} %turn_in.3), calls=%async_computation.2 | async-start | bytes 5505024 | tf_op jit(solution)/shard_map/all_to_all | solution.py:250
  15.4 63.5 %copy-start.5 = (s32[64]{0:T(128)S(1)}, s32[64]{0:T(128)}, u32[]{:S(2)}) copy-start(s32[64]{0:T(128)} %param.7) | copy-start | bytes 772
  73.0 1.6 copy-start
  74.6 66.4 %all-to-all-start = ((bf16[32,3,112,128]{3,2,1,0:T(8,128)(2,1)}), bf16[32,3,112,128]{3,2,1,0:T(8,128)(2,1)S(1)}, u32[]{:S(2)}, u32[]{:S(2)}) async-start(bf16[32,3,112,128]{3,2,1,0:T(8,128)(2,1)} %turn_in.2), calls=%async_computation | async-start | bytes 5505024 | tf_op jit(solution)/shard_map/all_to_all | solution.py:250
  80.2 1.8 copy-start.1
  100.0 0.9 copy-start.2
  141.0 26.9 %all-to-all-start.3 = ((bf16[32,112,128]{2,1,0:T(8,128)(2,1)}), bf16[32,112,128]{2,1,0:T(8,128)(2,1)}, u32[]{:S(2)}, u32[]{:S(2)}) async-start(bf16[32,112,128]{2,1,0:T(8,128)(2,1)} %copy-done.2), calls=%async_computation.3 | async-start | bytes 1835008 | tf_op jit(solution)/shard_map/all_to_all | solution.py:254
  162.6 1.0 copy-start.3
  167.9 26.8 %all-to-all-start.1 = ((bf16[32,112,128]{2,1,0:T(8,128)(2,1)}), bf16[32,112,128]{2,1,0:T(8,128)(2,1)S(1)}, u32[]{:S(2)}, u32[]{:S(2)}) async-start(bf16[32,112,128]{2,1,0:T(8,128)(2,1)} %copy-done.3), calls=%async_computation.1 | async-start | bytes 1835008 | tf_op jit(solution)/shard_map/all_to_all | solution.py:254
  194.6 0.9 copy-start.4

commit v3 on v2

--- a/solution.py
+++ b/solution.py
@@ -17,6 +17,7 @@
 LOG2E = 1.4426950408889634
 PIECE = 256
 SPAN = 100.0
+LOTS = 4
 
 
 def turn_in_kernel(q_ref, k_ref, v_ref, out_ref):
@@ -29,7 +30,7 @@
 
 def turn_in(query, key, value, first, heads, width):
     rows = query.shape[0]
-    step = LANES // math.gcd(width, LANES)
+    step = math.gcd(heads, 2 * LANES // math.gcd(width, LANES))
     start = first // step
     spec = pl.BlockSpec((rows, step * width), lambda i: (0, i + start))
     return pl.pallas_call(
@@ -45,24 +46,36 @@
     )(query, key, value)
 
 
-def turn_out_kernel(in_ref, *refs):
+def turn_out_kernel(first, in_ref, *refs):
+    out_ref, turned, sems = refs[-3:]
     heads, width, rows = in_ref.shape
-    refs[-1][...] = in_ref[...].reshape(heads * width, rows).T
+    lots, _, span = turned.shape
+    some = heads // lots
+    copies = []
+    for i in range(lots):
+        turned[i] = in_ref[i * some : (i + 1) * some].reshape(span, rows).T
+        columns = pl.ds(first * width + i * span, span)
+        copies.append(pltpu.make_async_copy(turned.at[i], out_ref.at[:, columns], sems.at[i]))
+        copies[-1].start()
+    for copy in copies:
+        copy.wait()
 
 
 def turn_out(parts, first, so_far, heads_total):
     heads, width, rows = parts.shape
-    step = LANES // math.gcd(width, LANES)
-    start = first // step
+    lots = math.gcd(LOTS, heads * width // LANES)
     given = () if so_far is None else (so_far,)
     return pl.pallas_call(
-        turn_out_kernel,
-        grid=(heads // step,),
-        in_specs=[pl.BlockSpec((step, width, rows), lambda i: (i, 0, 0))]
+        functools.partial(turn_out_kernel, first),
+        in_specs=[pl.BlockSpec(memory_space=pltpu.VMEM)]
         + [pl.BlockSpec(memory_space=pl.ANY)] * len(given),
-        out_specs=pl.BlockSpec((rows, step * width), lambda i: (0, i + start)),
+        out_specs=pl.BlockSpec(memory_space=pl.ANY),
         out_shape=jax.ShapeDtypeStruct((rows, heads_total * width), parts.dtype),
         input_output_aliases={1: 0} if given else {},
+        scratch_shapes=[
+            pltpu.VMEM((lots, rows, heads * width // lots), parts.dtype),
+            pltpu.SemaphoreType.DMA((lots,)),
+        ],
         cost_estimate=pl.CostEstimate(
             flops=0, transcendentals=0, bytes_accessed=4 * heads * width * rows
         ),
@@ -70,8 +83,15 @@
     )(parts, *given)
 
 
-def attend_kernel(sub, slope_ref, band_ref, qkv_ref, out_ref, keys, values):
-    blocks, _, width, rows = qkv_ref.shape
+def attend_kernel(sub, v_parts, parts_out, slope_ref, band_ref, given_ref, *refs):
+    v_refs, out_refs, refs = refs[:v_parts], refs[v_parts : v_parts + parts_out], refs[v_parts + parts_out :]
+    keys, values, refs = refs[0], refs[1], refs[2:]
+    blocks, _, width, rows = given_ref.shape
+    staged = refs if parts_out > 1 else ()
+    qkv_ref = staged[0] if staged else given_ref
+    out_ref = refs[-1] if parts_out > 1 else out_refs[0]
+    seq, slot = lax.axis_index("seq"), lax.axis_index("head")
+    slots = lax.axis_size("head")
     pad = LANES - width
     half = 2 * rows
     per = 2 * sub
@@ -93,11 +113,30 @@
             row == 0, high, jnp.where(row == 1, middle, jnp.where(row == 2, low, 0.0))
         ).astype(jnp.bfloat16)
         keys[pl.ds(at, rows), :] = jnp.concatenate([qkv_ref[block, 1], extra], axis=0).T
-        values[:width, pl.ds(at, rows)] = qkv_ref[block, 2]
+        if not v_parts:
+            values[:width, pl.ds(at, rows)] = qkv_ref[block, 2]
         values[width:, pl.ds(at, rows)] = jnp.ones((pad, rows), jnp.bfloat16)
         return carry
 
-    lax.fori_loop(0, blocks, fill, 0, unroll=4)
+    if staged:
+        lot = blocks // LOTS
+        copies = []
+        for i in range(LOTS):
+            some = pl.ds(i * lot, lot)
+            copies.append(
+                pltpu.make_async_copy(given_ref.at[some], qkv_ref.at[some], staged[1].at[i])
+            )
+            copies[-1].start()
+        for i in range(LOTS):
+            copies[i].wait()
+            lax.fori_loop(i * lot, (i + 1) * lot, fill, 0, unroll=4)
+    else:
+        lax.fori_loop(0, blocks, fill, 0, unroll=4)
+    for flip, ref in enumerate(v_refs):
+        for shift in range(slots):
+            block = (seq ^ flip) * slots + (slot + slots - shift) % slots
+            at = pl.multiple_of(block * rows, rows)
+            values[:width, pl.ds(at, rows)] = ref[shift]
     ones = jnp.ones((pad, half), jnp.bfloat16)
 
     def attend_tile(index, carry):
@@ -200,57 +239,275 @@
         return carry
 
     lax.fori_loop(0, blocks // per, attend_tile, 0)
-
-
-def attend(qkv, slope, band, heads_total):
-    blocks, _, width, rows = qkv.shape
+    if parts_out > 1:
+        for flip, ref in enumerate(out_refs):
+            ref[...] = out_ref[pl.ds((seq ^ flip) * slots, slots)]
+
+
+def attend(given, slope, band, values=(), parts_out=1):
+    blocks, _, width, rows = given.shape
     pairs = blocks * (blocks + 1) // 2
     sub = math.gcd(blocks, 8) // 2
-    return pl.pallas_call(
-        functools.partial(attend_kernel, sub),
+    shape = (blocks // parts_out, width, rows)
+    staged = [pltpu.VMEM(given.shape, given.dtype), pltpu.SemaphoreType.DMA((LOTS,))]
+    results = pl.pallas_call(
+        functools.partial(attend_kernel, sub, len(values), parts_out),
         in_specs=[
             pl.BlockSpec(memory_space=pltpu.SMEM),
             pl.BlockSpec(memory_space=pltpu.SMEM),
-            pl.BlockSpec(memory_space=pltpu.VMEM),
-        ],
-        out_specs=pl.BlockSpec(memory_space=pltpu.VMEM),
-        out_shape=jax.ShapeDtypeStruct((blocks, width, rows), jnp.bfloat16),
+            pl.BlockSpec(memory_space=pltpu.VMEM if parts_out == 1 else pl.ANY),
+        ]
+        + [pl.BlockSpec(memory_space=pltpu.VMEM)] * len(values),
+        out_specs=[pl.BlockSpec(memory_space=pltpu.VMEM)] * parts_out,
+        out_shape=[jax.ShapeDtypeStruct(shape, given.dtype)] * parts_out,
         scratch_shapes=[
-            pltpu.VMEM((blocks * rows, LANES), jnp.bfloat16),
-            pltpu.VMEM((LANES, blocks * rows), jnp.bfloat16),
-        ],
-        compiler_params=pltpu.CompilerParams(vmem_limit_bytes=32 * 2**20),
+            pltpu.VMEM((blocks * rows, LANES), given.dtype),
+            pltpu.VMEM((LANES, blocks * rows), given.dtype),
+        ]
+        + (staged if parts_out > 1 else [])
+        + ([pltpu.VMEM((blocks, width, rows), given.dtype)] if parts_out > 1 else []),
+        compiler_params=pltpu.CompilerParams(vmem_limit_bytes=28 * 2**20),
         cost_estimate=pl.CostEstimate(
             flops=4 * pairs * rows * rows * LANES,
             transcendentals=pairs * rows * rows,
             bytes_accessed=8 * blocks * width * rows,
         ),
         name="attend",
-    )(slope, band, qkv)
+    )(slope, band, given, *values)
+    return results if parts_out > 1 else results[0]
+
+
+def after(value, *others):
+    return lax.optimization_barrier((value, *others))[0]
+
+
+def moved(shapes, dtype, name, kernel, operands, scratch=(), where=None):
+    specs = where or [pl.BlockSpec(memory_space=pltpu.VMEM)] * len(operands)
+    size = 4 * sum(math.prod(shape) for shape in shapes)
+    return pl.pallas_call(
+        kernel,
+        in_specs=specs,
+        out_specs=[pl.BlockSpec(memory_space=pltpu.VMEM)] * len(shapes),
+        out_shape=[jax.ShapeDtypeStruct(shape, dtype) for shape in shapes],
+        scratch_shapes=list(scratch),
+        cost_estimate=pl.CostEstimate(flops=0, transcendentals=0, bytes_accessed=size),
+        name=name,
+    )(*operands)
+
+
+def cut_kernel(first, value_ref, *refs):
+    outs, sems = refs[:-1], refs[-1]
+    slot, slots = lax.axis_index("head"), lax.axis_size("head")
+    span = outs[0].shape[1]
+    copies = []
+    for i, out in enumerate(outs):
+        column = pl.multiple_of(first + ((slot + i + 1) % slots) * span, LANES)
+        copies.append(pltpu.make_async_copy(value_ref.at[:, pl.ds(column, span)], out, sems.at[i]))
+        copies[-1].start()
+    for copy in copies:
+        copy.wait()
+
+
+def cut(value, first, span):
+    slots = lax.axis_size("head")
+    return moved(
+        [(value.shape[0], span)] * (slots - 1),
+        value.dtype,
+        "cut",
+        functools.partial(cut_kernel, first),
+        [value],
+        [pltpu.SemaphoreType.DMA((slots - 1,))],
+        [pl.BlockSpec(memory_space=pl.ANY)],
+    )
+
+
+def turn_values_kernel(first, value_ref, *refs):
+    slot, slots = lax.axis_index("head"), lax.axis_size("head")
+    came, outs = refs[: slots - 1], refs[slots - 1 : -3]
+    own, turned, sem = refs[-3:]
+    span = own.shape[1]
+    width = outs[0].shape[1]
+    seq = lax.axis_index("seq")
+    column = pl.multiple_of(first + slot * span, LANES)
+    copy = pltpu.make_async_copy(value_ref.at[:, pl.ds(column, span)], own, sem)
+    copy.start()
+    for shift in [*range(1, slots), 0]:
+        if shift == 0:
+            copy.wait()
+        turned[...] = (own if shift == 0 else came[shift - 1])[...].T
+        for flip, out in enumerate(outs):
+            at = pl.multiple_of((seq ^ flip) * width, 16)
+            out[shift] = turned[pl.ds(at, width), :]
+
+
+def turn_values(value, came, first, width):
+    seqs, slots = lax.axis_size("seq"), lax.axis_size("head")
+    rows, span = came[0].shape
+    return moved(
+        [(slots, width, rows)] * seqs,
+        value.dtype,
+        "turn_values",
+        functools.partial(turn_values_kernel, first),
+        [value, *came],
+        [
+            pltpu.VMEM((rows, span), value.dtype),
+            pltpu.VMEM((span, rows), value.dtype),
+            pltpu.SemaphoreType.DMA(()),
+        ],
+        [pl.BlockSpec(memory_space=pl.ANY)] + [pl.BlockSpec(memory_space=pltpu.VMEM)] * len(came),
+    )
+
+
+def regroup_kernel(*refs):
+    seq, slot = lax.axis_index("seq"), lax.axis_index("head")
+    seqs, slots = lax.axis_size("seq"), lax.axis_size("head")
+    for flip in range(seqs):
+        for shift in range(slots):
+            refs[seqs + shift][seq ^ flip] = refs[flip][(slot + shift) % slots]
+
+
+def regroup(came):
+    seqs, slots = lax.axis_size("seq"), lax.axis_size("head")
+    shape = (seqs, *came[0].shape[1:])
+    return moved([shape] * slots, came[0].dtype, "regroup", regroup_kernel, came)
+
+
+def turn_in_slots_kernel(arrays, *refs):
+    out_ref = refs[-1]
+    seqs, slots, _, width, rows = out_ref.shape
+    for which in range(arrays):
+        turned = refs[which][...].T
+        for slot in range(slots):
+            for seq in range(seqs):
+                at = (slot * seqs + seq) * width
+                out_ref[seq, slot, which] = turned[at : at + width]
+
+
+def turn_in_slots(arrays, first, width):
+    seqs, slots = lax.axis_size("seq"), lax.axis_size("head")
+    rows = arrays[0].shape[0]
+    step = math.gcd(slots, 2)
+    start = first // (step * seqs)
+    spec = pl.BlockSpec((rows, step * seqs * width), lambda i: (0, i + start))
+    count = len(arrays)
+    out = pl.pallas_call(
+        functools.partial(turn_in_slots_kernel, count),
+        grid=(slots // step,),
+        in_specs=[spec] * count,
+        out_specs=pl.BlockSpec((seqs, step, count, width, rows), lambda i: (0, i, 0, 0, 0)),
+        out_shape=jax.ShapeDtypeStruct((seqs, slots, count, width, rows), arrays[0].dtype),
+        cost_estimate=pl.CostEstimate(
+            flops=0,
+            transcendentals=0,
+            bytes_accessed=4 * count * seqs * slots * width * rows,
+        ),
+        name="turn_in_slots",
+    )(*arrays)
+    return out.reshape(seqs * slots, count, width, rows)
+
+
+def turn_out_slots_kernel(first, parts, *refs):
+    out_ref, turned, sems = refs[-3:]
+    slots, rows, span = turned.shape
+    slot = lax.axis_index("head")
+    copies = []
+    for i in range(slots):
+        if parts == 1:
+            _, width, _ = refs[0].shape
+            heads = [refs[0][seq * slots + i] for seq in range(span // width)]
+            some, owner = jnp.concatenate(heads, axis=0), i
+        else:
+            some, owner = refs[i][...].reshape(span, rows), (slot + slots - i) % slots
+        turned[i] = some.T
+        columns = pl.ds(pl.multiple_of(first + owner * span, LANES), span)
+        copies.append(pltpu.make_async_copy(turned.at[i], out_ref.at[:, columns], sems.at[i]))
+        copies[-1].start()
+    for copy in copies:
+        copy.wait()
+
+
+def turn_out_slots(parts, first, so_far, width_total):
+    slots = lax.axis_size("head")
+    rows = parts[0].shape[-1]
+    span = sum(math.prod(part.shape[:-1]) for part in parts) // slots
+    given = () if so_far is None else (so_far,)
+    return pl.pallas_call(
+        functools.partial(turn_out_slots_kernel, first, len(parts)),
+        in_specs=[pl.BlockSpec(memory_space=pltpu.VMEM)] * len(parts)
+        + [pl.BlockSpec(memory_space=pl.ANY)] * len(given),
+        out_specs=pl.BlockSpec(memory_space=pl.ANY),
+        out_shape=jax.ShapeDtypeStruct((rows, width_total), parts[0].dtype),
+        input_output_aliases={len(parts): 0} if given else {},
+        scratch_shapes=[
+            pltpu.VMEM((slots, rows, span), parts[0].dtype),
+            pltpu.SemaphoreType.DMA((slots,)),
+        ],
+        cost_estimate=pl.CostEstimate(
+            flops=0, transcendentals=0, bytes_accessed=4 * slots * span * rows
+        ),
+        name="turn_out_slots",
+    )(*parts, *given)
+
+
+def in_two_sets(query, key, value, slope, band, width):
+    seqs, slots = lax.axis_size("seq"), lax.axis_size("head")
+    seq, slot = lax.axis_index("seq"), lax.axis_index("head")
+    half = seqs * slots
+    span = seqs * width
+
+    def send(x, flip, shift):
+        to = [
+            (s * slots + z, (s ^ flip) * slots + (z + shift) % slots)
+            for s in range(seqs)
+            for z in range(slots)
+        ]
+        return x if flip == shift == 0 else lax.ppermute(x, AXES, to)
+
+    def mine(first):
+        head = first + slot * seqs + seq
+        return [lax.dynamic_slice_in_dim(x, head, 1) for x in (slope, band)]
+
+    raw = (query, key, value)
+    given_a = lax.all_to_all(turn_in_slots(raw, 0, width), AXES, 0, 0, tiled=True)
+    given_b = lax.all_to_all(turn_in_slots(raw, half, width), AXES, 0, 0, tiled=True)
+
+    result_a = attend(given_a, *mine(0), parts_out=seqs)
+    groups = regroup([send(x, flip, 0) for flip, x in enumerate(result_a)])
+    *groups, given_b = lax.optimization_barrier((*groups, given_b))
+    back_a = [send(x, 0, shift) for shift, x in enumerate(groups)]
+
+    result_b = attend(given_b, *mine(half))
+    back_b = lax.all_to_all(after(result_b, *back_a[1:]), AXES, 0, 0, tiled=True)
+    out = turn_out_slots(back_a, 0, None, 2 * half * width)
+    return turn_out_slots([back_b], half * width, out, 2 * half * width)
 
 
 def on_device(query, key, value, exponent):
     rows, width_total = query.shape
     heads = exponent.shape[0]
     width = width_total // heads
-    devices = lax.axis_size("seq") * lax.axis_size("head")
-    me = lax.axis_index("seq") * lax.axis_size("head") + lax.axis_index("head")
+    seqs, slots = lax.axis_size("seq"), lax.axis_size("head")
+    devices = seqs * slots
+
+    band = MIN_BAND + (exponent - 1) * (MAX_BAND - MIN_BAND) // (heads - 1)
+    slope = jnp.exp2(-12.0 * exponent.astype(jnp.float32) / heads)
+
+    two_each = heads == 2 * devices and seqs & (seqs - 1) == 0 and slots % 2 == 0
+    if two_each and seqs * width % LANES == 0:
+        return in_two_sets(query, key, value, slope, band, width)
+
+    me = lax.axis_index("seq") * slots + lax.axis_index("head")
     share = max(1, devices // heads)
     owners = devices // share
-    rounds = heads // owners
-
-    band = MIN_BAND + (exponent - 1) * (MAX_BAND - MIN_BAND) // (heads - 1)
-    slope = jnp.exp2(-12.0 * exponent.astype(jnp.float32) / heads)
-
     out = None
-    for part in range(rounds):
+    for part in range(heads // owners):
         sent = turn_in(query, key, value, part * owners, owners, width)
         if share > 1:
             sent = jnp.repeat(sent, share, axis=0)
-        qkv = lax.all_to_all(sent, AXES, 0, 0, tiled=True)
+        given = lax.all_to_all(sent, AXES, 0, 0, tiled=True)
         head = part * owners + me // share
-        mine = lax.dynamic_slice_in_dim(slope, head, 1), lax.dynamic_slice_in_dim(band, head, 1)
-        result = attend(qkv, *mine, heads)
+        mine = [lax.dynamic_slice_in_dim(x, head, 1) for x in (slope, band)]
+        result = attend(given, *mine)
         back = lax.all_to_all(result, AXES, 0, 0, tiled=True)
         if share > 1:
             back = back.reshape(owners, share, width, rows)[:, 0]

time: 202 us -> 195 us (0.965)
  waiting for transfers between devices: 121 us -> 109 us
  starting transfers between devices: 19.3 us -> 23.2 us
    all_to_all x4 -> x3, waiting for transfers between devices: 121 us -> 97 us  [the longest x1 58.8 us: in_two_sets(): lax.all_to_all(turn_in_slots(raw, 0, width), AXES, 0, 0, tiled=True)]
    ppermute x0 -> x10, waiting for transfers between devices: none -> 11.7 us  [send(): return x if flip == shift == 0 else lax.ppermute(x, AXES, to)]
    ppermute x0 -> x10, starting transfers between devices: none -> 7.96 us  [send(): return x if flip == shift == 0 else lax.ppermute(x, AXES, to)]
    all_to_all x4 -> x3, starting transfers between devices: 19.3 us -> 15.2 us  [the longest x1 6.39 us: in_two_sets(): lax.all_to_all(turn_in_slots(raw, 0, width), AXES, 0, 0, tiled=True)]
    pallas_call x6 -> x7, Pallas kernels: 51.4 us -> 52.4 us  [the longest x2 39.1 us: attend(): pl.pallas_call(functools.partial(attend_kernel, sub, len(values), parts_o...]
    unnamed x12 -> x32, local copies, waits for them, and re-layouts: 6.18 us -> 6.56 us
  transfers between devices with their start and end apart: 4 -> 13, of which waited for: 4 -> 6; matrix products, arithmetic and copies ran while one was open for 1% -> 1% of each run, Pallas kernels for 22% -> 24%
where the time goes in v3:
time: 195 us; the launch traced here: 193 us
  waiting for transfers between devices  109 us (56%)
  Pallas kernels  52.4 us (27%)
  starting transfers between devices  23.2 us (12%)
  local copies, waits for them, and re-layouts  7.85 us (4%)
    all_to_all x1, waiting for transfers between devices, in_two_sets(): lax.all_to_all(turn_in_slots(raw, 0, width), AXES, 0, 0, tiled=True)  58.8 us
    pallas_call x2, Pallas kernels, attend(): pl.pallas_call(functools.partial(attend_kernel, sub, len(values), parts_o...  39.1 us
    all_to_all x1, waiting for transfers between devices, in_two_sets(): lax.all_to_all(after(result_b, *back_a[1:]), AXES, 0, 0, tiled=True)  20.1 us
    all_to_all x1, waiting for transfers between devices, in_two_sets(): lax.all_to_all(turn_in_slots(raw, half, width), AXES, 0, 0, tiled=True)  18.1 us
    ppermute x10, waiting for transfers between devices, send(): return x if flip == shift == 0 else lax.ppermute(x, AXES, to)  11.7 us
    ppermute x10, starting transfers between devices, send(): return x if flip == shift == 0 else lax.ppermute(x, AXES, to)  7.96 us
    unnamed x32, local copies, waits for them, and re-layouts  6.56 us
    pallas_call x2, Pallas kernels, turn_in_slots(): pl.pallas_call(functools.partial(turn_in_slots_kernel, count), grid=(slot...  6.53 us
  transfers between devices with their start and end apart: 13, of which 6 were waited for; matrix products, arithmetic and copies ran while one was open for 1% of the time, Pallas kernels for 24%

profile of v3, /device:TPU:7, one launch (start us, length us, event | category | flops | bytes accessed | tf_op | source)
XLA Modules:
  0.0 192.6 jit_solution(1106846067426246856)
XLA Ops:
  0.0 3.3 %turn_in_slots.2 = bf16[8,4,3,112,128]{4,3,2,1,0:T(8,128)(2,1)} custom-call(bf16[128,7168]{1,0:T(8,128)(2,1)} %refs_0_.3, bf16[128,7168]{1,0:T(8,128)(2,1)} %refs_1_.3, bf16[128,7168]{1,0:T(8,128)(2,1)} %refs_2_.3), custom_call_target="tpu_custom_call" | custom-call | bytes 5505024 | tf_op jit(solution)/shard_map/turn_in_slots/pallas_call | solution.py:393
  3.3 6.4 %all-to-all-start = ((bf16[32,3,112,128]{3,2,1,0:T(8,128)(2,1)}), bf16[32,3,112,128]{3,2,1,0:T(8,128)(2,1)S(1)}, u32[]{:S(2)}, u32[]{:S(2)}) async-start(bf16[32,3,112,128]{3,2,1,0:T(8,128)(2,1)} %bitcast.3), calls=%async_computation | async-start | bytes 5505024 | tf_op jit(solution)/shard_map/all_to_all | solution.py:471
  9.7 3.3 %turn_in_slots.3 = bf16[8,4,3,112,128]{4,3,2,1,0:T(8,128)(2,1)} custom-call(bf16[128,7168]{1,0:T(8,128)(2,1)} %refs_0_.3, bf16[128,7168]{1,0:T(8,128)(2,1)} %refs_1_.3, bf16[128,7168]{1,0:T(8,128)(2,1)} %refs_2_.3), custom_call_target="tpu_custom_call" | custom-call | bytes 5505024 | tf_op jit(solution)/shard_map/turn_in_slots/pallas_call | solution.py:393
  12.9 58.8 %all-to-all-done.given_ref = bf16[32,3,112,128]{3,2,1,0:T(8,128)(2,1)S(1)} async-done(((bf16[32,3,112,128]{3,2,1,0:T(8,128)(2,1)}), bf16[32,3,112,128]{3,2,1,0:T(8,128)(2,1)S(1)}, u32[]{:S(2)}, u32[]{:S(2)}) %all-to-all-start) | async-done | bytes 2752544 | tf_op jit(solution)/shard_map/all_to_all | solution.py:471
  71.8 1.6 copy-done
  73.3 4.3 %all-to-all-start.1 = ((bf16[32,3,112,128]{3,2,1,0:T(8,128)(2,1)}), bf16[32,3,112,128]{3,2,1,0:T(8,128)(2,1)S(1)}, u32[]{:S(2)}, u32[]{:S(2)}) async-start(bf16[32,3,112,128]{3,2,1,0:T(8,128)(2,1)} %bitcast.2), calls=%async_computation.1 | async-start | bytes 5505024 | tf_op jit(solution)/shard_map/all_to_all | solution.py:472
  79.0 1.8 copy-done.1
  80.7 20.9 %attend.2 = (bf16[4,112,128]{2,1,0:T(8,128)(2,1)S(1)}, bf16[4,112,128]{2,1,0:T(8,128)(2,1)S(1)}, bf16[4,112,128]{2,1,0:T(8,128)(2,1)S(1)}, bf16[4,112,128]{2,1,0...) custom-call(f32[1]{0:T(128)} %get-tuple-element.43.slope_ref, ...), custom_call_target="tpu_custom_call" | custom-call | flops 4429185024 | bytes 3670016 | tf_op jit(solution)/shard_map/attend/pallas_call | solution.py:253
  102.3 2.1 %collective-permute-start.2 = (bf16[4,112,128]{2,1,0:T(8,128)(2,1)S(1)}, bf16[4,112,128]{2,1,0:T(8,128)(2,1)S(1)}, u32[]{:S(2)}, u32[]{:S(2)}) collective-permute-start(bf16[4,112,128]{2,1,0:T(8,128)(2,1)S(1)} %get-tuple-element.26), channel_id=1, source_target_pairs={{0,12},{1,13},{2,14},{3,15},{4,8},{5,9},{6,10},{7,11},{8,4},{9,5},... | collective-permute-start | bytes 344072 | tf_op jit(solution)/shard_map/ppermute | solution.py:464
  104.4 1.4 collective-permute-start.4
  105.8 1.8 collective-permute-done.1.refs_2_
  107.6 1.2 collective-permute-start.6
  108.8 3.8 %collective-permute-done.2.refs_3_ = bf16[4,112,128]{2,1,0:T(8,128)(2,1)S(1)} collective-permute-done((bf16[4,112,128]{2,1,0:T(8,128)(2,1)S(1)}, bf16[4,112,128]{2,1,0:T(8,128)(2,1)S(1)}, u32[]{:S(2)}, u32[]{:S(2)}) %collective-permute-start.2) | collective-permute-done | bytes 114720 | tf_op jit(solution)/shard_map/ppermute | solution.py:464
  112.7 6.0 %collective-permute-done.4.refs_5_ = bf16[4,112,128]{2,1,0:T(8,128)(2,1)S(1)} collective-permute-done((bf16[4,112,128]{2,1,0:T(8,128)(2,1)S(1)}, bf16[4,112,128]{2,1,0:T(8,128)(2,1)S(1)}, u32[]{:S(2)}, u32[]{:S(2)}) %collective-permute-start.4) | collective-permute-done | bytes 114720 | tf_op jit(solution)/shard_map/ppermute | solution.py:464
  119.4 2.2 %regroup.1 = (bf16[8,112,128]{2,1,0:T(8,128)(2,1)}, bf16[8,112,128]{2,1,0:T(8,128)(2,1)}, bf16[8,112,128]{2,1,0:T(8,128)(2,1)}, bf16[8,112,128]{2,1,0:T(8,128)(2,1)}) custom-call(bf16[4,112,128]{2,1,0:T(8,128)(2,1)} %copy-done.3, bf16[4,112,128]{2,1,0:T(8,128)(2,1)} %copy-done.8, bf16[4,112,128]{2,1,0:T(8,128)(2,1)} %copy-done.9, ...), custom_call_target="tpu_custom_call" | custom-call | bytes 1835008 | tf_op jit(solution)/shard_map/regroup/pallas_call | solution.py:287
  121.7 18.1 %all-to-all-done.1.given_ref = bf16[32,3,112,128]{3,2,1,0:T(8,128)(2,1)S(1)} async-done(((bf16[32,3,112,128]{3,2,1,0:T(8,128)(2,1)}), bf16[32,3,112,128]{3,2,1,0:T(8,128)(2,1)S(1)}, u32[]{:S(2)}, u32[]{:S(2)}) %all-to-all-start.1) | async-done | bytes 2752544 | tf_op jit(solution)/shard_map/all_to_all | solution.py:472
  140.5 2.5 %collective-permute-start.9 = (bf16[8,112,128]{2,1,0:T(8,128)(2,1)}, bf16[8,112,128]{2,1,0:T(8,128)(2,1)S(1)}, u32[]{:S(2)}, u32[]{:S(2)}) collective-permute-start(bf16[8,112,128]{2,1,0:T(8,128)(2,1)} %get-tuple-element.38), channel_id=1, source_target_pairs={{0,3},{1,0},{2,1},{3,2},{4,7},{5,4},{6,5},{7,6},{8,11},{9,8},{10,9... | collective-permute-start | bytes 688136 | tf_op jit(solution)/shard_map/ppermute | solution.py:464
  143.0 18.2 %attend.3 = bf16[32,112,128]{2,1,0:T(8,128)(2,1)S(1)} custom-call(f32[1]{0:T(128)} %get-tuple-element.44.slope_ref, s32[1]{0:T(128)} %get-tuple-element.42.band_ref, bf16[32,3,112,128]{3,2,1,0:T(8,128)(2,1)S(1)} %all-to-all-done.1.given_ref), custom_call_target="tpu_custom_call" | custom-call | flops 4429185024 | bytes 3670016 | tf_op jit(solution)/shard_map/attend/pallas_call | solution.py:253
  161.2 0.9 copy-done.2
  162.2 4.5 %all-to-all-start.2 = ((bf16[32,112,128]{2,1,0:T(8,128)(2,1)}), bf16[32,112,128]{2,1,0:T(8,128)(2,1)S(1)}, u32[]{:S(2)}, u32[]{:S(2)}) async-start(bf16[32,112,128]{2,1,0:T(8,128)(2,1)} %copy-done.2), calls=%async_computation.2 | async-start | bytes 1835008 | tf_op jit(solution)/shard_map/all_to_all | solution.py:480
  166.8 2.4 %turn_out_slots.2.refs_1_ = bf16[128,7168]{1,0:T(8,128)(2,1)} custom-call(bf16[8,112,128]{2,1,0:T(8,128)(2,1)} %get-tuple-element.40.refs_0_, bf16[8,112,128]{2,1,0:T(8,128)(2,1)} %copy-done.5, bf16[8,112,128]{2,1,0:T(8,128)(2,1)} %copy-done.6, bf16[8,112,128]{2,1,0:T(8,128)(2,1)} %copy-done.7), custom_call_target="tpu_custom_call" | custom-call | bytes 1835008 | tf_op jit(solution)/shard_map/turn_out_slots/pallas_call | solution.py:434
  169.1 20.1 %all-to-all-done.2.refs_0_ = bf16[32,112,128]{2,1,0:T(8,128)(2,1)S(1)} async-done(((bf16[32,112,128]{2,1,0:T(8,128)(2,1)}), bf16[32,112,128]{2,1,0:T(8,128)(2,1)S(1)}, u32[]{:S(2)}, u32[]{:S(2)}) %all-to-all-start.2) | async-done | bytes 917536 | tf_op jit(solution)/shard_map/all_to_all | solution.py:480
  189.2 0.9 copy-done.4
  190.2 2.2 %turn_out_slots.3 = bf16[128,7168]{1,0:T(8,128)(2,1)} custom-call(bf16[32,112,128]{2,1,0:T(8,128)(2,1)} %copy-done.4, bf16[128,7168]{1,0:T(8,128)(2,1)} %turn_out_slots.2.refs_1_), custom_call_target="tpu_custom_call", output_to_operand_aliasing={{}: (1, {})} | custom-call | bytes 1835008 | tf_op jit(solution)/shard_map/turn_out_slots/pallas_call | solution.py:434
  (45 shorter events, 3.4 us)
Async XLA Ops:
  3.3 68.5 %all-to-all-start = ((bf16[32,3,112,128]{3,2,1,0:T(8,128)(2,1)}), bf16[32,3,112,128]{3,2,1,0:T(8,128)(2,1)S(1)}, u32[]{:S(2)}, u32[]{:S(2)}) async-start(bf16[32,3,112,128]{3,2,1,0:T(8,128)(2,1)} %bitcast.3), calls=%async_computation | async-start | bytes 5505024 | tf_op jit(solution)/shard_map/all_to_all | solution.py:471
  71.8 1.6 copy-start
  73.3 4.3 %copy-start.15 = (s32[64]{0:T(128)S(1)}, s32[64]{0:T(128)}, u32[]{:S(2)}) copy-start(s32[64]{0:T(128)} %param.7) | copy-start | bytes 772
  73.3 66.4 %all-to-all-start.1 = ((bf16[32,3,112,128]{3,2,1,0:T(8,128)(2,1)}), bf16[32,3,112,128]{3,2,1,0:T(8,128)(2,1)S(1)}, u32[]{:S(2)}, u32[]{:S(2)}) async-start(bf16[32,3,112,128]{3,2,1,0:T(8,128)(2,1)} %bitcast.2), calls=%async_computation.1 | async-start | bytes 5505024 | tf_op jit(solution)/shard_map/all_to_all | solution.py:472
  79.0 1.8 copy-start.1
  102.3 3.5 %collective-permute-start = (bf16[4,112,128]{2,1,0:T(8,128)(2,1)S(1)}, bf16[4,112,128]{2,1,0:T(8,128)(2,1)S(1)}, u32[]{:S(2)}, u32[]{:S(2)}) collective-permute-start(bf16[4,112,128]{2,1,0:T(8,128)(2,1)S(1)} %get-tuple-element.24), channel_id=1, source_target_pairs={{0,4},{1,5},{2,6},{3,7},{4,0},{5,1},{6,2},{7,3},{8,12},{9,13},{10,... | collective-permute-start | bytes 344072 | tf_op jit(solution)/shard_map/ppermute | solution.py:464
  102.3 5.3 %collective-permute-start.1 = (bf16[4,112,128]{2,1,0:T(8,128)(2,1)S(1)}, bf16[4,112,128]{2,1,0:T(8,128)(2,1)S(1)}, u32[]{:S(2)}, u32[]{:S(2)}) collective-permute-start(bf16[4,112,128]{2,1,0:T(8,128)(2,1)S(1)} %get-tuple-element.25), channel_id=1, source_target_pairs={{0,8},{1,9},{2,10},{3,11},{4,12},{5,13},{6,14},{7,15},{8,0},{9,1},... | collective-permute-start | bytes 344072 | tf_op jit(solution)/shard_map/ppermute | solution.py:464
  102.3 10.4 %collective-permute-start.2 = (bf16[4,112,128]{2,1,0:T(8,128)(2,1)S(1)}, bf16[4,112,128]{2,1,0:T(8,128)(2,1)S(1)}, u32[]{:S(2)}, u32[]{:S(2)}) collective-permute-start(bf16[4,112,128]{2,1,0:T(8,128)(2,1)S(1)} %get-tuple-element.26), channel_id=1, source_target_pairs={{0,12},{1,13},{2,14},{3,15},{4,8},{5,9},{6,10},{7,11},{8,4},{9,5},... | collective-permute-start | bytes 344072 | tf_op jit(solution)/shard_map/ppermute | solution.py:464
  104.4 8.2 %collective-permute-start.3 = (bf16[4,112,128]{2,1,0:T(8,128)(2,1)S(1)}, bf16[4,112,128]{2,1,0:T(8,128)(2,1)S(1)}, u32[]{:S(2)}, u32[]{:S(2)}) collective-permute-start(bf16[4,112,128]{2,1,0:T(8,128)(2,1)S(1)} %get-tuple-element.27), channel_id=1, source_target_pairs={{0,16},{1,17},{2,18},{3,19},{4,20},{5,21},{6,22},{7,23},{8,24},{9,... | collective-permute-start | bytes 344072 | tf_op jit(solution)/shard_map/ppermute | solution.py:464
  104.4 14.3 %collective-permute-start.4 = (bf16[4,112,128]{2,1,0:T(8,128)(2,1)S(1)}, bf16[4,112,128]{2,1,0:T(8,128)(2,1)S(1)}, u32[]{:S(2)}, u32[]{:S(2)}) collective-permute-start(bf16[4,112,128]{2,1,0:T(8,128)(2,1)S(1)} %get-tuple-element.28), channel_id=1, source_target_pairs={{0,20},{1,21},{2,22},{3,23},{4,16},{5,17},{6,18},{7,19},{8,28},{9,... | collective-permute-start | bytes 344072 | tf_op jit(solution)/shard_map/ppermute | solution.py:464
  105.8 13.0 %copy-start.8 = (bf16[4,112,128]{2,1,0:T(8,128)(2,1)}, bf16[4,112,128]{2,1,0:T(8,128)(2,1)S(1)}, u32[]{:S(2)}) copy-start(bf16[4,112,128]{2,1,0:T(8,128)(2,1)S(1)} %collective-permute-done.refs_1_) | copy-start | bytes 344068
  105.8 12.9 %collective-permute-start.5 = (bf16[4,112,128]{2,1,0:T(8,128)(2,1)S(1)}, bf16[4,112,128]{2,1,0:T(8,128)(2,1)S(1)}, u32[]{:S(2)}, u32[]{:S(2)}) collective-permute-start(bf16[4,112,128]{2,1,0:T(8,128)(2,1)S(1)} %get-tuple-element.29), channel_id=1, source_target_pairs={{0,24},{1,25},{2,26},{3,27},{4,28},{5,29},{6,30},{7,31},{8,16},{9,... | collective-permute-start | bytes 344072 | tf_op jit(solution)/shard_map/ppermute | solution.py:464
  107.6 11.1 %copy-start.9 = (bf16[4,112,128]{2,1,0:T(8,128)(2,1)}, bf16[4,112,128]{2,1,0:T(8,128)(2,1)S(1)}, u32[]{:S(2)}) copy-start(bf16[4,112,128]{2,1,0:T(8,128)(2,1)S(1)} %collective-permute-done.1.refs_2_) | copy-start | bytes 344068
  107.6 11.1 %collective-permute-start.6 = (bf16[4,112,128]{2,1,0:T(8,128)(2,1)S(1)}, bf16[4,112,128]{2,1,0:T(8,128)(2,1)S(1)}, u32[]{:S(2)}, u32[]{:S(2)}) collective-permute-start(bf16[4,112,128]{2,1,0:T(8,128)(2,1)S(1)} %get-tuple-element.30), channel_id=1, source_target_pairs={{0,28},{1,29},{2,30},{3,31},{4,24},{5,25},{6,26},{7,27},{8,20},{9,... | collective-permute-start | bytes 344072 | tf_op jit(solution)/shard_map/ppermute | solution.py:464
  112.7 6.1 %copy-start.10 = (bf16[4,112,128]{2,1,0:T(8,128)(2,1)}, bf16[4,112,128]{2,1,0:T(8,128)(2,1)S(1)}, u32[]{:S(2)}) copy-start(bf16[4,112,128]{2,1,0:T(8,128)(2,1)S(1)} %collective-permute-done.2.refs_3_) | copy-start | bytes 344068
  112.7 6.1 %copy-start.11 = (bf16[4,112,128]{2,1,0:T(8,128)(2,1)}, bf16[4,112,128]{2,1,0:T(8,128)(2,1)S(1)}, u32[]{:S(2)}) copy-start(bf16[4,112,128]{2,1,0:T(8,128)(2,1)S(1)} %collective-permute-done.3.refs_4_) | copy-start | bytes 344068
  139.7 22.4 %collective-permute-start.7 = (bf16[8,112,128]{2,1,0:T(8,128)(2,1)}, bf16[8,112,128]{2,1,0:T(8,128)(2,1)S(1)}, u32[]{:S(2)}, u32[]{:S(2)}) collective-permute-start(bf16[8,112,128]{2,1,0:T(8,128)(2,1)} %get-tuple-element.36), channel_id=1, source_target_pairs={{0,1},{1,2},{2,3},{3,0},{4,5},{5,6},{6,7},{7,4},{8,9},{9,10},{10,1... | collective-permute-start | bytes 688136 | tf_op jit(solution)/shard_map/ppermute | solution.py:464
  140.5 21.7 %collective-permute-start.8 = (bf16[8,112,128]{2,1,0:T(8,128)(2,1)}, bf16[8,112,128]{2,1,0:T(8,128)(2,1)S(1)}, u32[]{:S(2)}, u32[]{:S(2)}) collective-permute-start(bf16[8,112,128]{2,1,0:T(8,128)(2,1)} %get-tuple-element.37), channel_id=1, source_target_pairs={{0,2},{1,3},{2,0},{3,1},{4,6},{5,7},{6,4},{7,5},{8,10},{9,11},{10,... | collective-permute-start | bytes 688136 | tf_op jit(solution)/shard_map/ppermute | solution.py:464
  140.5 21.7 %collective-permute-start.9 = (bf16[8,112,128]{2,1,0:T(8,128)(2,1)}, bf16[8,112,128]{2,1,0:T(8,128)(2,1)S(1)}, u32[]{:S(2)}, u32[]{:S(2)}) collective-permute-start(bf16[8,112,128]{2,1,0:T(8,128)(2,1)} %get-tuple-element.38), channel_id=1, source_target_pairs={{0,3},{1,0},{2,1},{3,2},{4,7},{5,4},{6,5},{7,6},{8,11},{9,8},{10,9... | collective-permute-start | bytes 688136 | tf_op jit(solution)/shard_map/ppermute | solution.py:464
  161.2 0.9 copy-start.2
  162.1 4.6 %copy-start.5 = (bf16[8,112,128]{2,1,0:T(8,128)(2,1)}, bf16[8,112,128]{2,1,0:T(8,128)(2,1)S(1)}, u32[]{:S(2)}) copy-start(bf16[8,112,128]{2,1,0:T(8,128)(2,1)S(1)} %collective-permute-done.7.refs_1_) | copy-start | bytes 688132
  162.2 4.6 %copy-start.6 = (bf16[8,112,128]{2,1,0:T(8,128)(2,1)}, bf16[8,112,128]{2,1,0:T(8,128)(2,1)S(1)}, u32[]{:S(2)}) copy-start(bf16[8,112,128]{2,1,0:T(8,128)(2,1)S(1)} %collective-permute-done.8.refs_2_) | copy-start | bytes 688132
  162.2 4.6 %copy-start.7 = (bf16[8,112,128]{2,1,0:T(8,128)(2,1)}, bf16[8,112,128]{2,1,0:T(8,128)(2,1)S(1)}, u32[]{:S(2)}) copy-start(bf16[8,112,128]{2,1,0:T(8,128)(2,1)S(1)} %collective-permute-done.9.refs_3_) | copy-start | bytes 688132
  162.2 27.0 %all-to-all-start.2 = ((bf16[32,112,128]{2,1,0:T(8,128)(2,1)}), bf16[32,112,128]{2,1,0:T(8,128)(2,1)S(1)}, u32[]{:S(2)}, u32[]{:S(2)}) async-start(bf16[32,112,128]{2,1,0:T(8,128)(2,1)} %copy-done.2), calls=%async_computation.2 | async-start | bytes 1835008 | tf_op jit(solution)/shard_map/all_to_all | solution.py:480
  (5 other events, 3.7 us)

commit v4 on v3

--- a/solution.py
+++ b/solution.py
@@ -16,7 +16,9 @@
 DEAD = -1e30
 LOG2E = 1.4426950408889634
 PIECE = 256
-SPAN = 100.0
+SPAN = 90.0
+BESIDE = 400
+WHOLE_VMEM = 62 * 2**20
 LOTS = 4
 
 
@@ -85,7 +87,7 @@
 
 def attend_kernel(sub, v_parts, parts_out, slope_ref, band_ref, given_ref, *refs):
     v_refs, out_refs, refs = refs[:v_parts], refs[v_parts : v_parts + parts_out], refs[v_parts + parts_out :]
-    keys, values, refs = refs[0], refs[1], refs[2:]
+    queries, keys, values, refs = refs[0], refs[1], refs[2], refs[3:]
     blocks, _, width, rows = given_ref.shape
     staged = refs if parts_out > 1 else ()
     qkv_ref = staged[0] if staged else given_ref
@@ -109,10 +111,14 @@
         rest = bias - high
         middle = rest.astype(jnp.bfloat16).astype(jnp.float32)
         low = rest - middle
-        extra = jnp.where(
-            row == 0, high, jnp.where(row == 1, middle, jnp.where(row == 2, low, 0.0))
-        ).astype(jnp.bfloat16)
-        keys[pl.ds(at, rows), :] = jnp.concatenate([qkv_ref[block, 1], extra], axis=0).T
+        part = jnp.where(
+            (row == 0) | (row == 3), high, jnp.where((row == 1) | (row == 4), middle, low)
+        )
+        for_key = jnp.where(row < 3, part, jnp.where(row < 6, 1.0, 0.0)).astype(jnp.bfloat16)
+        for_query = jnp.where(row < 3, 1.0, jnp.where(row < 6, -part, 0.0)).astype(jnp.bfloat16)
+        keys[pl.ds(at, rows), :] = jnp.concatenate([qkv_ref[block, 1], for_key], axis=0).T
+        queries[:width, pl.ds(at, rows)] = qkv_ref[block, 0]
+        queries[width:, pl.ds(at, rows)] = for_query
         if not v_parts:
             values[:width, pl.ds(at, rows)] = qkv_ref[block, 2]
         values[width:, pl.ds(at, rows)] = jnp.ones((pad, rows), jnp.bfloat16)
@@ -137,23 +143,25 @@
             block = (seq ^ flip) * slots + (slot + slots - shift) % slots
             at = pl.multiple_of(block * rows, rows)
             values[:width, pl.ds(at, rows)] = ref[shift]
-    ones = jnp.ones((pad, half), jnp.bfloat16)
-
-    def attend_tile(index, carry):
+
+    def attend_tile(fast, index, carry):
         first = per * index
 
         def query_of(s):
-            pair = [qkv_ref[first + 2 * s, 0], qkv_ref[first + 2 * s + 1, 0]]
-            return jnp.concatenate([jnp.concatenate(pair, axis=1), ones], axis=0)
-
-        def live(start, count, s):
-            key_pos = start + lax.broadcasted_iota(jnp.int32, (count, half), 0)
-            query_pos = (first + 2 * s) * rows + lax.broadcasted_iota(jnp.int32, (count, half), 1)
-            return (query_pos >= key_pos) & (query_pos // BLOCK - key_pos // BLOCK < band)
+            return queries[:, pl.ds(pl.multiple_of((first + 2 * s) * rows, half), half)]
 
         def scored(start, count, s, masked, query):
             score = jnp.dot(keys[pl.ds(start, count), :], query, preferred_element_type=jnp.float32)
-            return jnp.where(live(start, count, s), score, DEAD) if masked else score
+            if not masked:
+                return score
+            key = lax.broadcasted_iota(jnp.int32, (count, half), 0)
+            token = lax.broadcasted_iota(jnp.int32, (count, half), 1)
+            if masked == "diagonal":
+                live = token + (count - half) >= key
+            else:
+                ahead = (first + 2 * s) * rows - start
+                live = (ahead // BLOCK + token // BLOCK) - key // BLOCK < band
+            return jnp.where(live, score, DEAD)
 
         def weighed(start, count, weights):
             return jnp.dot(
@@ -170,75 +178,77 @@
             shrink = jnp.exp2((top - new_top) * factor)
             return new_top, total * shrink + weighed(start, count, weights)
 
-        def fast_step(start, count, s, masked, query, state):
-            top, total, high = state
-            pieces = []
-            for at in range(0, count, PIECE):
-                score = scored(start + at, PIECE, s, masked, query)
-                pieces.append(jnp.exp2(score * factor - top * factor).astype(jnp.bfloat16))
-                high = jnp.maximum(high, jnp.max(score.reshape(PIECE // 8, 8, half), axis=0))
-            return top, total + weighed(start, count, jnp.concatenate(pieces, axis=0)), high
+        def fast_steps(start, counts, masked, query, states):
+            pieces = [[] for _ in range(sub)]
+            highs = [high for _, high in states]
+            for at in range(0, max(counts), PIECE):
+                for s in range(sub):
+                    if at >= counts[s]:
+                        continue
+                    mask = masked
+                    if masked == "diagonal" and at + PIECE < counts[s]:
+                        mask = False
+                    score = scored(start + at, PIECE, s, mask, query[s])
+                    pieces[s].append(jnp.exp2(score * factor).astype(jnp.bfloat16))
+                    top = jnp.max(score.reshape(PIECE // 8, 8, half), axis=0)
+                    highs[s] = jnp.maximum(highs[s], top)
+            weights = [jnp.concatenate(pieces[s], axis=0) for s in range(sub)]
+            return [
+                (states[s][0] + weighed(start, counts[s], weights[s]), highs[s])
+                for s in range(sub)
+            ]
 
         whole = jnp.minimum(first, band - per) // per
         needed = jnp.minimum(first, band - 1)
         rest = (needed - per * whole + per - 1) // per
 
-        def sweep(step, queries, states):
-            def steps(masked):
-                def body(j, states):
+        def sweep(steps, states):
+            def body(masked):
+                def some(j, states):
                     start = pl.multiple_of((first - per * (j + 1)) * rows, half)
-                    return [
-                        step(start, per * rows, s, masked, queries[s], states[s])
-                        for s in range(sub)
-                    ]
-
-                return body
-
-            states = lax.fori_loop(0, whole, steps(False), states)
-            return lax.fori_loop(whole, whole + rest, steps(True), states)
+                    return steps(start, [per * rows] * sub, masked, query, states)
+
+                return some
+
+            states = lax.fori_loop(0, whole, body(False), states)
+            return lax.fori_loop(whole, whole + rest, body("band"), states)
 
         def finish(s, total):
             result = (total[:width] / total[width : width + 1]).astype(jnp.bfloat16)
             out_ref[first + 2 * s] = result[:, :rows]
             out_ref[first + 2 * s + 1] = result[:, rows:]
 
-        queries = [query_of(s) for s in range(sub)]
-        states = []
+        def slow_steps(start, counts, masked, query, states):
+            return [
+                slow_step(start, counts[s], s, masked, query[s], states[s]) for s in range(sub)
+            ]
+
+        query = [query_of(s) for s in range(sub)]
+        start = pl.multiple_of(first * rows, half)
+        counts = [half * (s + 1) for s in range(sub)]
+        nothing = jnp.zeros((LANES, half), jnp.float32)
+        if fast:
+            steps = fast_steps
+            states = [(nothing, jnp.full((8, half), DEAD, jnp.float32))] * sub
+        else:
+            steps = slow_steps
+            states = [(jnp.full((1, half), DEAD, jnp.float32), nothing)] * sub
+        states = steps(start, counts, "diagonal", query, states)
+        states = sweep(steps, states)
         for s in range(sub):
-            start = pl.multiple_of((first + 2 * s) * rows, half)
-            score = scored(start, half, s, True, queries[s])
-            top = jnp.max(score, axis=0, keepdims=True)
-            total = weighed(start, half, jnp.exp2(score * factor - top * factor))
-            state = (top, total, jnp.full((8, half), DEAD, jnp.float32))
-            if s:
-                start = pl.multiple_of(first * rows, half)
-                state = fast_step(start, half * s, s, False, queries[s], state)
-            states.append(state)
-        states = sweep(fast_step, queries, states)
-        worst = jnp.float32(DEAD)
-        for s in range(sub):
-            top, total, high = states[s]
-            finish(s, total)
-            worst = jnp.maximum(worst, jnp.max(high - top))
-
-        @pl.when(worst * factor > SPAN)
-        def _():
-            queries = [query_of(s) for s in range(sub)]
-            states = []
-            for s in range(sub):
-                state = (
-                    jnp.full((1, half), DEAD, jnp.float32),
-                    jnp.zeros((LANES, half), jnp.float32),
-                )
-                start = pl.multiple_of(first * rows, half)
-                states.append(slow_step(start, half * (s + 1), s, True, queries[s], state))
-            states = sweep(slow_step, queries, states)
-            for s in range(sub):
-                finish(s, states[s][1])
-
+            finish(s, states[s][0 if fast else 1])
+            if fast:
+                high = jnp.max(states[s][1], axis=0, keepdims=True)
+                carry = jnp.maximum(carry, jnp.abs(high))
         return carry
 
-    lax.fori_loop(0, blocks // per, attend_tile, 0)
+    worst = jnp.zeros((1, half), jnp.float32)
+    worst = lax.fori_loop(0, blocks // per, functools.partial(attend_tile, True), worst)
+
+    @pl.when(jnp.max(worst) * factor > SPAN)
+    def _():
+        lax.fori_loop(0, blocks // per, functools.partial(attend_tile, False), 0)
+
     if parts_out > 1:
         for flip, ref in enumerate(out_refs):
             ref[...] = out_ref[pl.ds((seq ^ flip) * slots, slots)]
@@ -261,6 +271,7 @@
         out_specs=[pl.BlockSpec(memory_space=pltpu.VMEM)] * parts_out,
         out_shape=[jax.ShapeDtypeStruct(shape, given.dtype)] * parts_out,
         scratch_shapes=[
+            pltpu.VMEM((LANES, blocks * rows), given.dtype),
             pltpu.VMEM((blocks * rows, LANES), given.dtype),
             pltpu.VMEM((LANES, blocks * rows), given.dtype),
         ]
@@ -401,6 +412,7 @@
             transcendentals=0,
             bytes_accessed=4 * count * seqs * slots * width * rows,
         ),
+        compiler_params=pltpu.CompilerParams(vmem_limit_bytes=WHOLE_VMEM),
         name="turn_in_slots",
     )(*arrays)
     return out.reshape(seqs * slots, count, width, rows)
@@ -443,7 +455,9 @@
             pltpu.SemaphoreType.DMA((slots,)),
         ],
         cost_estimate=pl.CostEstimate(
-            flops=0, transcendentals=0, bytes_accessed=4 * slots * span * rows
+            flops=0 if so_far is not None else BESIDE * 10**9,
+            transcendentals=0,
+            bytes_accessed=4 * slots * span * rows,
         ),
         name="turn_out_slots",
     )(*parts, *given)
@@ -477,7 +491,7 @@
     back_a = [send(x, 0, shift) for shift, x in enumerate(groups)]
 
     result_b = attend(given_b, *mine(half))
-    back_b = lax.all_to_all(after(result_b, *back_a[1:]), AXES, 0, 0, tiled=True)
+    back_b = lax.all_to_all(result_b, AXES, 0, 0, tiled=True)
     out = turn_out_slots(back_a, 0, None, 2 * half * width)
     return turn_out_slots([back_b], half * width, out, 2 * half * width)
 

time: 195 us -> 219 us (1.12)
  Pallas kernels: 52.4 us -> 94.4 us
  waiting for transfers between devices: 109 us -> 91.2 us
  local copies, waits for them, and re-layouts: 7.85 us -> 5 us
  starting transfers between devices: 23.2 us -> 25.6 us
    pallas_call x2, Pallas kernels: 39.1 us -> 81 us  [attend(): pl.pallas_call(functools.partial(attend_kernel, sub, len(values), parts_o...]
    all_to_all x1, waiting for transfers between devices: 18.1 us -> 0.01 us  [in_two_sets(): lax.all_to_all(turn_in_slots(raw, half, width), AXES, 0, 0, tiled=True)]
    unnamed x32 -> x26, local copies, waits for them, and re-layouts: 6.56 us -> 3.71 us
  transfers between devices with their start and end apart: 13 -> 13, of which waited for: 6 -> 5; matrix products, arithmetic and copies ran while one was open for 1% -> 1% of each run, Pallas kernels for 24% -> 41%
where the time goes in v4:
time: 219 us; the launch traced here: 217 us
  Pallas kernels  94.4 us (43%)
  waiting for transfers between devices  91.2 us (42%)
  starting transfers between devices  25.6 us (12%)
  local copies, waits for them, and re-layouts  5 us (2%)
    pallas_call x2, Pallas kernels, attend(): pl.pallas_call(functools.partial(attend_kernel, sub, len(values), parts_o...  81 us
    all_to_all x1, waiting for transfers between devices, in_two_sets(): lax.all_to_all(turn_in_slots(raw, 0, width), AXES, 0, 0, tiled=True)  58.9 us
    all_to_all x1, waiting for transfers between devices, in_two_sets(): back_b = lax.all_to_all(result_b, AXES, 0, 0, tiled=True)  18.8 us
    ppermute x10, waiting for transfers between devices, send(): return x if flip == shift == 0 else lax.ppermute(x, AXES, to)  13.6 us
    ppermute x10, starting transfers between devices, send(): return x if flip == shift == 0 else lax.ppermute(x, AXES, to)  8.22 us
    all_to_all x1, starting transfers between devices, in_two_sets(): back_b = lax.all_to_all(result_b, AXES, 0, 0, tiled=True)  6.65 us
    pallas_call x2, Pallas kernels, turn_in_slots(): pl.pallas_call(functools.partial(turn_in_slots_kernel, count), grid=(slot...  6.54 us
    all_to_all x1, starting transfers between devices, in_two_sets(): lax.all_to_all(turn_in_slots(raw, 0, width), AXES, 0, 0, tiled=True)  6.43 us
  transfers between devices with their start and end apart: 13, of which 5 were waited for; matrix products, arithmetic and copies ran while one was open for 1% of the time, Pallas kernels for 41%

profile of v4, /device:TPU:7, one launch (start us, length us, event | category | flops | bytes accessed | tf_op | source)
XLA Modules:
  0.0 216.6 jit_solution(7737110004339969448)
XLA Ops:
  0.0 3.3 %turn_in_slots.2 = bf16[8,4,3,112,128]{4,3,2,1,0:T(8,128)(2,1)} custom-call(bf16[128,7168]{1,0:T(8,128)(2,1)} %refs_0_.3, bf16[128,7168]{1,0:T(8,128)(2,1)} %refs_1_.3, bf16[128,7168]{1,0:T(8,128)(2,1)} %refs_2_.3), custom_call_target="tpu_custom_call" | custom-call | bytes 5505024 | tf_op jit(solution)/shard_map/turn_in_slots/pallas_call | solution.py:404
  3.3 6.4 %all-to-all-start = ((bf16[32,3,112,128]{3,2,1,0:T(8,128)(2,1)}), bf16[32,3,112,128]{3,2,1,0:T(8,128)(2,1)}, u32[]{:S(2)}, u32[]{:S(2)}) async-start(bf16[32,3,112,128]{3,2,1,0:T(8,128)(2,1)} %bitcast.3), calls=%async_computation | async-start | bytes 5505024 | tf_op jit(solution)/shard_map/all_to_all | solution.py:485
  9.7 3.3 %turn_in_slots.3 = bf16[8,4,3,112,128]{4,3,2,1,0:T(8,128)(2,1)} custom-call(bf16[128,7168]{1,0:T(8,128)(2,1)} %refs_0_.3, bf16[128,7168]{1,0:T(8,128)(2,1)} %refs_1_.3, bf16[128,7168]{1,0:T(8,128)(2,1)} %refs_2_.3), custom_call_target="tpu_custom_call" | custom-call | bytes 5505024 | tf_op jit(solution)/shard_map/turn_in_slots/pallas_call | solution.py:404
  13.0 58.9 %all-to-all-done.given_ref = bf16[32,3,112,128]{3,2,1,0:T(8,128)(2,1)} async-done(((bf16[32,3,112,128]{3,2,1,0:T(8,128)(2,1)}), bf16[32,3,112,128]{3,2,1,0:T(8,128)(2,1)}, u32[]{:S(2)}, u32[]{:S(2)}) %all-to-all-start) | async-done | bytes 2752544 | tf_op jit(solution)/shard_map/all_to_all | solution.py:485
  71.9 4.3 %all-to-all-start.1 = ((bf16[32,3,112,128]{3,2,1,0:T(8,128)(2,1)}), bf16[32,3,112,128]{3,2,1,0:T(8,128)(2,1)S(1)}, u32[]{:S(2)}, u32[]{:S(2)}) async-start(bf16[32,3,112,128]{3,2,1,0:T(8,128)(2,1)} %bitcast.2), calls=%async_computation.1 | async-start | bytes 5505024 | tf_op jit(solution)/shard_map/all_to_all | solution.py:486
  76.8 0.7 fusion.1
  77.5 42.1 %attend.2 = (bf16[4,112,128]{2,1,0:T(8,128)(2,1)S(1)}, bf16[4,112,128]{2,1,0:T(8,128)(2,1)S(1)}, bf16[4,112,128]{2,1,0:T(8,128)(2,1)S(1)}, bf16[4,112,128]{2,1,0...) custom-call(f32[1]{0:T(128)} %get-tuple-element.41.slope_ref, ...), custom_call_target="tpu_custom_call" | custom-call | flops 4429185024 | bytes 3670016 | tf_op jit(solution)/shard_map/attend/pallas_call | solution.py:263
  120.5 1.9 collective-permute-start.2
  122.4 1.4 collective-permute-start.4
  123.9 3.4 %collective-permute-done.1.refs_2_ = bf16[4,112,128]{2,1,0:T(8,128)(2,1)S(1)} collective-permute-done((bf16[4,112,128]{2,1,0:T(8,128)(2,1)S(1)}, bf16[4,112,128]{2,1,0:T(8,128)(2,1)S(1)}, u32[]{:S(2)}, u32[]{:S(2)}) %collective-permute-start.1) | collective-permute-done | bytes 114720 | tf_op jit(solution)/shard_map/ppermute | solution.py:478
  127.3 0.8 collective-permute-start.6
  128.2 2.5 %collective-permute-done.2.refs_3_ = bf16[4,112,128]{2,1,0:T(8,128)(2,1)S(1)} collective-permute-done((bf16[4,112,128]{2,1,0:T(8,128)(2,1)S(1)}, bf16[4,112,128]{2,1,0:T(8,128)(2,1)S(1)}, u32[]{:S(2)}, u32[]{:S(2)}) %collective-permute-start.2) | collective-permute-done | bytes 114720 | tf_op jit(solution)/shard_map/ppermute | solution.py:478
  130.7 7.6 %collective-permute-done.4.refs_5_ = bf16[4,112,128]{2,1,0:T(8,128)(2,1)S(1)} collective-permute-done((bf16[4,112,128]{2,1,0:T(8,128)(2,1)S(1)}, bf16[4,112,128]{2,1,0:T(8,128)(2,1)S(1)}, u32[]{:S(2)}, u32[]{:S(2)}) %collective-permute-start.4) | collective-permute-done | bytes 114720 | tf_op jit(solution)/shard_map/ppermute | solution.py:478
  139.1 2.2 %regroup.1 = (bf16[8,112,128]{2,1,0:T(8,128)(2,1)}, bf16[8,112,128]{2,1,0:T(8,128)(2,1)}, bf16[8,112,128]{2,1,0:T(8,128)(2,1)}, bf16[8,112,128]{2,1,0:T(8,128)(2,1)}) custom-call(bf16[4,112,128]{2,1,0:T(8,128)(2,1)} %copy-done.1, bf16[4,112,128]{2,1,0:T(8,128)(2,1)} %copy-done.2, bf16[4,112,128]{2,1,0:T(8,128)(2,1)} %copy-done.3, ...), custom_call_target="tpu_custom_call" | custom-call | bytes 1835008 | tf_op jit(solution)/shard_map/regroup/pallas_call | solution.py:298
  141.3 1.1 collective-permute-start.7
  142.4 1.3 collective-permute-start.8
  143.7 1.3 collective-permute-start.9
  145.0 38.9 %attend.3 = bf16[32,112,128]{2,1,0:T(8,128)(2,1)S(1)} custom-call(f32[1]{0:T(128)} %get-tuple-element.42.slope_ref, s32[1]{0:T(128)} %get-tuple-element.40.band_ref, bf16[32,3,112,128]{3,2,1,0:T(8,128)(2,1)S(1)} %all-to-all-done.1.given_ref), custom_call_target="tpu_custom_call" | custom-call | flops 4429185024 | bytes 3670016 | tf_op jit(solution)/shard_map/attend/pallas_call | solution.py:263
  184.0 0.9 copy-done
  184.9 6.6 %all-to-all-start.2 = ((bf16[32,112,128]{2,1,0:T(8,128)(2,1)}), bf16[32,112,128]{2,1,0:T(8,128)(2,1)}, u32[]{:S(2)}, u32[]{:S(2)}) async-start(bf16[32,112,128]{2,1,0:T(8,128)(2,1)} %copy-done), calls=%async_computation.2 | async-start | bytes 1835008 | tf_op jit(solution)/shard_map/all_to_all | solution.py:494
  192.3 0.7 copy-done.11
  193.0 2.3 %turn_out_slots.2.refs_1_ = bf16[128,7168]{1,0:T(8,128)(2,1)} custom-call(bf16[8,112,128]{2,1,0:T(8,128)(2,1)} %get-tuple-element.35.refs_0_, bf16[8,112,128]{2,1,0:T(8,128)(2,1)} %copy-done.9, bf16[8,112,128]{2,1,0:T(8,128)(2,1)} %copy-done.10, bf16[8,112,128]{2,1,0:T(8,128)(2,1)} %copy-done.11), custom_call_target="tpu_custom_call" | custom-call | flops 399999991808 | bytes 1835008 | tf_op jit(solution)/shard_map/turn_out_slots/pallas_call | solution.py:446
  195.4 18.8 %all-to-all-done.2.refs_0_ = bf16[32,112,128]{2,1,0:T(8,128)(2,1)} async-done(((bf16[32,112,128]{2,1,0:T(8,128)(2,1)}), bf16[32,112,128]{2,1,0:T(8,128)(2,1)}, u32[]{:S(2)}, u32[]{:S(2)}) %all-to-all-start.2) | async-done | bytes 917536 | tf_op jit(solution)/shard_map/all_to_all | solution.py:494
  214.2 2.2 %turn_out_slots.3 = bf16[128,7168]{1,0:T(8,128)(2,1)} custom-call(bf16[32,112,128]{2,1,0:T(8,128)(2,1)} %all-to-all-done.2.refs_0_, bf16[128,7168]{1,0:T(8,128)(2,1)} %turn_out_slots.2.refs_1_), custom_call_target="tpu_custom_call", output_to_operand_aliasing={{}: (1, {})} | custom-call | bytes 1835008 | tf_op jit(solution)/shard_map/turn_out_slots/pallas_call | solution.py:446
  (39 shorter events, 3.2 us)
Async XLA Ops:
  3.3 68.6 %all-to-all-start = ((bf16[32,3,112,128]{3,2,1,0:T(8,128)(2,1)}), bf16[32,3,112,128]{3,2,1,0:T(8,128)(2,1)}, u32[]{:S(2)}, u32[]{:S(2)}) async-start(bf16[32,3,112,128]{3,2,1,0:T(8,128)(2,1)} %bitcast.3), calls=%async_computation | async-start | bytes 5505024 | tf_op jit(solution)/shard_map/all_to_all | solution.py:485
  71.9 4.3 %copy-start.12 = (s32[64]{0:T(128)S(1)}, s32[64]{0:T(128)}, u32[]{:S(2)}) copy-start(s32[64]{0:T(128)} %param.7) | copy-start | bytes 772
  71.9 69.4 %all-to-all-start.1 = ((bf16[32,3,112,128]{3,2,1,0:T(8,128)(2,1)}), bf16[32,3,112,128]{3,2,1,0:T(8,128)(2,1)S(1)}, u32[]{:S(2)}, u32[]{:S(2)}) async-start(bf16[32,3,112,128]{3,2,1,0:T(8,128)(2,1)} %bitcast.2), calls=%async_computation.1 | async-start | bytes 5505024 | tf_op jit(solution)/shard_map/all_to_all | solution.py:486
  120.2 3.5 %collective-permute-start = (bf16[4,112,128]{2,1,0:T(8,128)(2,1)S(1)}, bf16[4,112,128]{2,1,0:T(8,128)(2,1)S(1)}, u32[]{:S(2)}, u32[]{:S(2)}) collective-permute-start(bf16[4,112,128]{2,1,0:T(8,128)(2,1)S(1)} %get-tuple-element.23), channel_id=1, source_target_pairs={{0,4},{1,5},{2,6},{3,7},{4,0},{5,1},{6,2},{7,3},{8,12},{9,13},{10,... | collective-permute-start | bytes 344072 | tf_op jit(solution)/shard_map/ppermute | solution.py:478
  120.2 7.1 %collective-permute-start.1 = (bf16[4,112,128]{2,1,0:T(8,128)(2,1)S(1)}, bf16[4,112,128]{2,1,0:T(8,128)(2,1)S(1)}, u32[]{:S(2)}, u32[]{:S(2)}) collective-permute-start(bf16[4,112,128]{2,1,0:T(8,128)(2,1)S(1)} %get-tuple-element.24), channel_id=1, source_target_pairs={{0,8},{1,9},{2,10},{3,11},{4,12},{5,13},{6,14},{7,15},{8,0},{9,1},... | collective-permute-start | bytes 344072 | tf_op jit(solution)/shard_map/ppermute | solution.py:478
  120.5 10.2 %collective-permute-start.2 = (bf16[4,112,128]{2,1,0:T(8,128)(2,1)S(1)}, bf16[4,112,128]{2,1,0:T(8,128)(2,1)S(1)}, u32[]{:S(2)}, u32[]{:S(2)}) collective-permute-start(bf16[4,112,128]{2,1,0:T(8,128)(2,1)S(1)} %get-tuple-element.25), channel_id=1, source_target_pairs={{0,12},{1,13},{2,14},{3,15},{4,8},{5,9},{6,10},{7,11},{8,4},{9,5},... | collective-permute-start | bytes 344072 | tf_op jit(solution)/shard_map/ppermute | solution.py:478
  122.4 8.3 %collective-permute-start.3 = (bf16[4,112,128]{2,1,0:T(8,128)(2,1)S(1)}, bf16[4,112,128]{2,1,0:T(8,128)(2,1)S(1)}, u32[]{:S(2)}, u32[]{:S(2)}) collective-permute-start(bf16[4,112,128]{2,1,0:T(8,128)(2,1)S(1)} %get-tuple-element.26), channel_id=1, source_target_pairs={{0,16},{1,17},{2,18},{3,19},{4,20},{5,21},{6,22},{7,23},{8,24},{9,... | collective-permute-start | bytes 344072 | tf_op jit(solution)/shard_map/ppermute | solution.py:478
  122.4 15.9 %collective-permute-start.4 = (bf16[4,112,128]{2,1,0:T(8,128)(2,1)S(1)}, bf16[4,112,128]{2,1,0:T(8,128)(2,1)S(1)}, u32[]{:S(2)}, u32[]{:S(2)}) collective-permute-start(bf16[4,112,128]{2,1,0:T(8,128)(2,1)S(1)} %get-tuple-element.27), channel_id=1, source_target_pairs={{0,20},{1,21},{2,22},{3,23},{4,16},{5,17},{6,18},{7,19},{8,28},{9,... | collective-permute-start | bytes 344072 | tf_op jit(solution)/shard_map/ppermute | solution.py:478
  123.7 14.6 %copy-start.2 = (bf16[4,112,128]{2,1,0:T(8,128)(2,1)}, bf16[4,112,128]{2,1,0:T(8,128)(2,1)S(1)}, u32[]{:S(2)}) copy-start(bf16[4,112,128]{2,1,0:T(8,128)(2,1)S(1)} %collective-permute-done.refs_1_) | copy-start | bytes 344068
  123.7 14.6 %collective-permute-start.5 = (bf16[4,112,128]{2,1,0:T(8,128)(2,1)S(1)}, bf16[4,112,128]{2,1,0:T(8,128)(2,1)S(1)}, u32[]{:S(2)}, u32[]{:S(2)}) collective-permute-start(bf16[4,112,128]{2,1,0:T(8,128)(2,1)S(1)} %get-tuple-element.28), channel_id=1, source_target_pairs={{0,24},{1,25},{2,26},{3,27},{4,28},{5,29},{6,30},{7,31},{8,16},{9,... | collective-permute-start | bytes 344072 | tf_op jit(solution)/shard_map/ppermute | solution.py:478
  127.3 11.0 %copy-start.3 = (bf16[4,112,128]{2,1,0:T(8,128)(2,1)}, bf16[4,112,128]{2,1,0:T(8,128)(2,1)S(1)}, u32[]{:S(2)}) copy-start(bf16[4,112,128]{2,1,0:T(8,128)(2,1)S(1)} %collective-permute-done.1.refs_2_) | copy-start | bytes 344068
  127.3 11.0 %collective-permute-start.6 = (bf16[4,112,128]{2,1,0:T(8,128)(2,1)S(1)}, bf16[4,112,128]{2,1,0:T(8,128)(2,1)S(1)}, u32[]{:S(2)}, u32[]{:S(2)}) collective-permute-start(bf16[4,112,128]{2,1,0:T(8,128)(2,1)S(1)} %get-tuple-element.29), channel_id=1, source_target_pairs={{0,28},{1,29},{2,30},{3,31},{4,24},{5,25},{6,26},{7,27},{8,20},{9,... | collective-permute-start | bytes 344072 | tf_op jit(solution)/shard_map/ppermute | solution.py:478
  130.7 7.7 %copy-start.4 = (bf16[4,112,128]{2,1,0:T(8,128)(2,1)}, bf16[4,112,128]{2,1,0:T(8,128)(2,1)S(1)}, u32[]{:S(2)}) copy-start(bf16[4,112,128]{2,1,0:T(8,128)(2,1)S(1)} %collective-permute-done.2.refs_3_) | copy-start | bytes 344068
  130.7 7.7 %copy-start.5 = (bf16[4,112,128]{2,1,0:T(8,128)(2,1)}, bf16[4,112,128]{2,1,0:T(8,128)(2,1)S(1)}, u32[]{:S(2)}) copy-start(bf16[4,112,128]{2,1,0:T(8,128)(2,1)S(1)} %collective-permute-done.3.refs_4_) | copy-start | bytes 344068
  138.3 0.7 copy-start.7
  138.3 0.7 copy-start.8
  141.3 50.3 %collective-permute-start.7 = (bf16[8,112,128]{2,1,0:T(8,128)(2,1)}, bf16[8,112,128]{2,1,0:T(8,128)(2,1)S(1)}, u32[]{:S(2)}, u32[]{:S(2)}) collective-permute-start(bf16[8,112,128]{2,1,0:T(8,128)(2,1)} %get-tuple-element.36), channel_id=1, source_target_pairs={{0,1},{1,2},{2,3},{3,0},{4,5},{5,6},{6,7},{7,4},{8,9},{9,10},{10,1... | collective-permute-start | bytes 688136 | tf_op jit(solution)/shard_map/ppermute | solution.py:478
  142.4 49.2 %collective-permute-start.8 = (bf16[8,112,128]{2,1,0:T(8,128)(2,1)}, bf16[8,112,128]{2,1,0:T(8,128)(2,1)S(1)}, u32[]{:S(2)}, u32[]{:S(2)}) collective-permute-start(bf16[8,112,128]{2,1,0:T(8,128)(2,1)} %get-tuple-element.37), channel_id=1, source_target_pairs={{0,2},{1,3},{2,0},{3,1},{4,6},{5,7},{6,4},{7,5},{8,10},{9,11},{10,... | collective-permute-start | bytes 688136 | tf_op jit(solution)/shard_map/ppermute | solution.py:478
  143.7 47.9 %collective-permute-start.9 = (bf16[8,112,128]{2,1,0:T(8,128)(2,1)}, bf16[8,112,128]{2,1,0:T(8,128)(2,1)S(1)}, u32[]{:S(2)}, u32[]{:S(2)}) collective-permute-start(bf16[8,112,128]{2,1,0:T(8,128)(2,1)} %get-tuple-element.38), channel_id=1, source_target_pairs={{0,3},{1,0},{2,1},{3,2},{4,7},{5,4},{6,5},{7,6},{8,11},{9,8},{10,9... | collective-permute-start | bytes 688136 | tf_op jit(solution)/shard_map/ppermute | solution.py:478
  183.9 0.9 copy-start
  184.9 29.3 %all-to-all-start.2 = ((bf16[32,112,128]{2,1,0:T(8,128)(2,1)}), bf16[32,112,128]{2,1,0:T(8,128)(2,1)}, u32[]{:S(2)}, u32[]{:S(2)}) async-start(bf16[32,112,128]{2,1,0:T(8,128)(2,1)} %copy-done), calls=%async_computation.2 | async-start | bytes 1835008 | tf_op jit(solution)/shard_map/all_to_all | solution.py:494
  191.6 0.7 copy-start.9
  191.6 0.8 copy-start.10
  192.3 0.7 copy-start.11
  (2 other events, 1.3 us)

commit v5 on v4

--- a/solution.py
+++ b/solution.py
@@ -214,7 +214,7 @@
             return lax.fori_loop(whole, whole + rest, body("band"), states)
 
         def finish(s, total):
-            result = (total[:width] / total[width : width + 1]).astype(jnp.bfloat16)
+            result = (total[:width] * (1.0 / total[width : width + 1])).astype(jnp.bfloat16)
             out_ref[first + 2 * s] = result[:, :rows]
             out_ref[first + 2 * s + 1] = result[:, rows:]
 
@@ -487,7 +487,8 @@
 
     result_a = attend(given_a, *mine(0), parts_out=seqs)
     groups = regroup([send(x, flip, 0) for flip, x in enumerate(result_a)])
-    *groups, given_b = lax.optimization_barrier((*groups, given_b))
+    held, given_b = lax.optimization_barrier((groups[2], given_b))
+    groups = [*groups[:2], held, *groups[3:]]
     back_a = [send(x, 0, shift) for shift, x in enumerate(groups)]
 
     result_b = attend(given_b, *mine(half))

time: 219 us -> 219 us (level)
  starting transfers between devices: 25.6 us -> 30.7 us
  Pallas kernels: 94.4 us -> 90.2 us
    ppermute x10, starting transfers between devices: 8.22 us -> 14 us  [send(): return x if flip == shift == 0 else lax.ppermute(x, AXES, to)]
    pallas_call x2, Pallas kernels: 81 us -> 76.8 us  [attend(): pl.pallas_call(functools.partial(attend_kernel, sub, len(values), parts_o...]
  transfers between devices with their start and end apart: 13 -> 13, of which waited for: 5 -> 5; matrix products, arithmetic and copies ran while one was open for 1% -> 1% of each run, Pallas kernels for 41% -> 39%
where the time goes in v5:
time: 219 us; the launch traced here: 216 us
  waiting for transfers between devices  90.8 us (41%)
  Pallas kernels  90.2 us (41%)
  starting transfers between devices  30.7 us (14%)
  local copies, waits for them, and re-layouts  4.38 us (2%)
    pallas_call x2, Pallas kernels, attend(): pl.pallas_call(functools.partial(attend_kernel, sub, len(values), parts_o...  76.8 us
    all_to_all x1, waiting for transfers between devices, in_two_sets(): lax.all_to_all(turn_in_slots(raw, 0, width), AXES, 0, 0, tiled=True)  58.9 us
    all_to_all x1, waiting for transfers between devices, in_two_sets(): back_b = lax.all_to_all(result_b, AXES, 0, 0, tiled=True)  19.4 us
    ppermute x10, starting transfers between devices, send(): return x if flip == shift == 0 else lax.ppermute(x, AXES, to)  14 us
    ppermute x10, waiting for transfers between devices, send(): return x if flip == shift == 0 else lax.ppermute(x, AXES, to)  12.5 us
    pallas_call x2, Pallas kernels, turn_in_slots(): pl.pallas_call(functools.partial(turn_in_slots_kernel, count), grid=(slot...  6.54 us
    all_to_all x1, starting transfers between devices, in_two_sets(): lax.all_to_all(turn_in_slots(raw, 0, width), AXES, 0, 0, tiled=True)  6.43 us
    all_to_all x1, starting transfers between devices, in_two_sets(): back_b = lax.all_to_all(result_b, AXES, 0, 0, tiled=True)  5.98 us
  transfers between devices with their start and end apart: 13, of which 5 were waited for; matrix products, arithmetic and copies ran while one was open for 1% of the time, Pallas kernels for 39%

profile of v5, /device:TPU:7, one launch (start us, length us, event | category | flops | bytes accessed | tf_op | source)
XLA Modules:
  0.0 216.4 jit_solution(5523944374375939116)
XLA Ops:
  0.0 3.3 %turn_in_slots.2 = bf16[8,4,3,112,128]{4,3,2,1,0:T(8,128)(2,1)} custom-call(bf16[128,7168]{1,0:T(8,128)(2,1)} %refs_0_.3, bf16[128,7168]{1,0:T(8,128)(2,1)} %refs_1_.3, bf16[128,7168]{1,0:T(8,128)(2,1)} %refs_2_.3), custom_call_target="tpu_custom_call" | custom-call | bytes 5505024 | tf_op jit(solution)/shard_map/turn_in_slots/pallas_call | solution.py:404
  3.3 6.4 %all-to-all-start = ((bf16[32,3,112,128]{3,2,1,0:T(8,128)(2,1)}), bf16[32,3,112,128]{3,2,1,0:T(8,128)(2,1)}, u32[]{:S(2)}, u32[]{:S(2)}) async-start(bf16[32,3,112,128]{3,2,1,0:T(8,128)(2,1)} %bitcast.3), calls=%async_computation | async-start | bytes 5505024 | tf_op jit(solution)/shard_map/all_to_all | solution.py:485
  9.7 3.3 %turn_in_slots.3 = bf16[8,4,3,112,128]{4,3,2,1,0:T(8,128)(2,1)} custom-call(bf16[128,7168]{1,0:T(8,128)(2,1)} %refs_0_.3, bf16[128,7168]{1,0:T(8,128)(2,1)} %refs_1_.3, bf16[128,7168]{1,0:T(8,128)(2,1)} %refs_2_.3), custom_call_target="tpu_custom_call" | custom-call | bytes 5505024 | tf_op jit(solution)/shard_map/turn_in_slots/pallas_call | solution.py:404
  13.0 58.9 %all-to-all-done.given_ref = bf16[32,3,112,128]{3,2,1,0:T(8,128)(2,1)} async-done(((bf16[32,3,112,128]{3,2,1,0:T(8,128)(2,1)}), bf16[32,3,112,128]{3,2,1,0:T(8,128)(2,1)}, u32[]{:S(2)}, u32[]{:S(2)}) %all-to-all-start) | async-done | bytes 2752544 | tf_op jit(solution)/shard_map/all_to_all | solution.py:485
  71.9 4.3 %all-to-all-start.1 = ((bf16[32,3,112,128]{3,2,1,0:T(8,128)(2,1)}), bf16[32,3,112,128]{3,2,1,0:T(8,128)(2,1)S(1)}, u32[]{:S(2)}, u32[]{:S(2)}) async-start(bf16[32,3,112,128]{3,2,1,0:T(8,128)(2,1)} %bitcast.2), calls=%async_computation.1 | async-start | bytes 5505024 | tf_op jit(solution)/shard_map/all_to_all | solution.py:486
  76.8 0.7 fusion.1
  77.5 37.4 %attend.2 = (bf16[4,112,128]{2,1,0:T(8,128)(2,1)S(1)}, bf16[4,112,128]{2,1,0:T(8,128)(2,1)S(1)}, bf16[4,112,128]{2,1,0:T(8,128)(2,1)S(1)}, bf16[4,112,128]{2,1,0...) custom-call(f32[1]{0:T(128)} %get-tuple-element.35.slope_ref, ...), custom_call_target="tpu_custom_call" | custom-call | flops 4429185024 | bytes 3670016 | tf_op jit(solution)/shard_map/attend/pallas_call | solution.py:263
  115.9 4.6 %collective-permute-start.1 = (bf16[4,112,128]{2,1,0:T(8,128)(2,1)S(1)}, bf16[4,112,128]{2,1,0:T(8,128)(2,1)S(1)}, u32[]{:S(2)}, u32[]{:S(2)}) collective-permute-start(bf16[4,112,128]{2,1,0:T(8,128)(2,1)S(1)} %get-tuple-element.21), channel_id=1, source_target_pairs={{0,8},{1,9},{2,10},{3,11},{4,12},{5,13},{6,14},{7,15},{8,0},{9,1},... | collective-permute-start | bytes 344072 | tf_op jit(solution)/shard_map/ppermute | solution.py:478
  121.0 2.0 collective-permute-start.4
  123.0 1.0 collective-permute-start.5
  123.9 2.7 %collective-permute-done.1.refs_2_ = bf16[4,112,128]{2,1,0:T(8,128)(2,1)S(1)} collective-permute-done((bf16[4,112,128]{2,1,0:T(8,128)(2,1)S(1)}, bf16[4,112,128]{2,1,0:T(8,128)(2,1)S(1)}, u32[]{:S(2)}, u32[]{:S(2)}) %collective-permute-start.1) | collective-permute-done | bytes 114720 | tf_op jit(solution)/shard_map/ppermute | solution.py:478
  126.6 3.5 %collective-permute-done.2.refs_3_ = bf16[4,112,128]{2,1,0:T(8,128)(2,1)S(1)} collective-permute-done((bf16[4,112,128]{2,1,0:T(8,128)(2,1)S(1)}, bf16[4,112,128]{2,1,0:T(8,128)(2,1)S(1)}, u32[]{:S(2)}, u32[]{:S(2)}) %collective-permute-start.2) | collective-permute-done | bytes 114720 | tf_op jit(solution)/shard_map/ppermute | solution.py:478
  130.2 6.2 %collective-permute-done.4.refs_5_ = bf16[4,112,128]{2,1,0:T(8,128)(2,1)S(1)} collective-permute-done((bf16[4,112,128]{2,1,0:T(8,128)(2,1)S(1)}, bf16[4,112,128]{2,1,0:T(8,128)(2,1)S(1)}, u32[]{:S(2)}, u32[]{:S(2)}) %collective-permute-start.4) | collective-permute-done | bytes 114720 | tf_op jit(solution)/shard_map/ppermute | solution.py:478
  137.2 2.2 %regroup.1 = (bf16[8,112,128]{2,1,0:T(8,128)(2,1)}, bf16[8,112,128]{2,1,0:T(8,128)(2,1)}, bf16[8,112,128]{2,1,0:T(8,128)(2,1)}, bf16[8,112,128]{2,1,0:T(8,128)(2,1)}) custom-call(bf16[4,112,128]{2,1,0:T(8,128)(2,1)} %copy-done.1, bf16[4,112,128]{2,1,0:T(8,128)(2,1)} %copy-done.2, bf16[4,112,128]{2,1,0:T(8,128)(2,1)} %copy-done.3, ...), custom_call_target="tpu_custom_call" | custom-call | bytes 1835008 | tf_op jit(solution)/shard_map/regroup/pallas_call | solution.py:298
  139.4 3.0 %collective-permute-start.7 = (bf16[8,112,128]{2,1,0:T(8,128)(2,1)}, bf16[8,112,128]{2,1,0:T(8,128)(2,1)S(1)}, u32[]{:S(2)}, u32[]{:S(2)}) collective-permute-start(bf16[8,112,128]{2,1,0:T(8,128)(2,1)} %get-tuple-element.30), channel_id=1, source_target_pairs={{0,1},{1,2},{2,3},{3,0},{4,5},{5,6},{6,7},{7,4},{8,9},{9,10},{10,1... | collective-permute-start | bytes 688136 | tf_op jit(solution)/shard_map/ppermute | solution.py:478
  142.4 1.2 collective-permute-start.8
  143.6 1.3 collective-permute-start.9
  145.0 39.5 %attend.3 = bf16[32,112,128]{2,1,0:T(8,128)(2,1)S(1)} custom-call(f32[1]{0:T(128)} %get-tuple-element.36.slope_ref, s32[1]{0:T(128)} %get-tuple-element.34.band_ref, bf16[32,3,112,128]{3,2,1,0:T(8,128)(2,1)S(1)} %all-to-all-done.1.given_ref), custom_call_target="tpu_custom_call" | custom-call | flops 4429185024 | bytes 3670016 | tf_op jit(solution)/shard_map/attend/pallas_call | solution.py:263
  184.5 0.9 copy-done
  185.4 6.0 %all-to-all-start.2 = ((bf16[32,112,128]{2,1,0:T(8,128)(2,1)}), bf16[32,112,128]{2,1,0:T(8,128)(2,1)}, u32[]{:S(2)}, u32[]{:S(2)}) async-start(bf16[32,112,128]{2,1,0:T(8,128)(2,1)} %copy-done), calls=%async_computation.2 | async-start | bytes 1835008 | tf_op jit(solution)/shard_map/all_to_all | solution.py:495
  191.5 0.6 copy-done.9
  192.3 2.3 %turn_out_slots.2.refs_1_ = bf16[128,7168]{1,0:T(8,128)(2,1)} custom-call(bf16[8,112,128]{2,1,0:T(8,128)(2,1)} %get-tuple-element.29.refs_0_, bf16[8,112,128]{2,1,0:T(8,128)(2,1)} %copy-done.9, bf16[8,112,128]{2,1,0:T(8,128)(2,1)} %copy-done.10, bf16[8,112,128]{2,1,0:T(8,128)(2,1)} %copy-done.11), custom_call_target="tpu_custom_call" | custom-call | flops 399999991808 | bytes 1835008 | tf_op jit(solution)/shard_map/turn_out_slots/pallas_call | solution.py:446
  194.6 19.4 %all-to-all-done.2.refs_0_ = bf16[32,112,128]{2,1,0:T(8,128)(2,1)} async-done(((bf16[32,112,128]{2,1,0:T(8,128)(2,1)}), bf16[32,112,128]{2,1,0:T(8,128)(2,1)}, u32[]{:S(2)}, u32[]{:S(2)}) %all-to-all-start.2) | async-done | bytes 917536 | tf_op jit(solution)/shard_map/all_to_all | solution.py:495
  214.0 2.2 %turn_out_slots.3 = bf16[128,7168]{1,0:T(8,128)(2,1)} custom-call(bf16[32,112,128]{2,1,0:T(8,128)(2,1)} %all-to-all-done.2.refs_0_, bf16[128,7168]{1,0:T(8,128)(2,1)} %turn_out_slots.2.refs_1_), custom_call_target="tpu_custom_call", output_to_operand_aliasing={{}: (1, {})} | custom-call | bytes 1835008 | tf_op jit(solution)/shard_map/turn_out_slots/pallas_call | solution.py:446
  (39 shorter events, 3.0 us)
Async XLA Ops:
  3.3 68.6 %all-to-all-start = ((bf16[32,3,112,128]{3,2,1,0:T(8,128)(2,1)}), bf16[32,3,112,128]{3,2,1,0:T(8,128)(2,1)}, u32[]{:S(2)}, u32[]{:S(2)}) async-start(bf16[32,3,112,128]{3,2,1,0:T(8,128)(2,1)} %bitcast.3), calls=%async_computation | async-start | bytes 5505024 | tf_op jit(solution)/shard_map/all_to_all | solution.py:485
  71.9 4.3 %copy-start.12 = (s32[64]{0:T(128)S(1)}, s32[64]{0:T(128)}, u32[]{:S(2)}) copy-start(s32[64]{0:T(128)} %param.7) | copy-start | bytes 772
  71.9 67.5 %all-to-all-start.1 = ((bf16[32,3,112,128]{3,2,1,0:T(8,128)(2,1)}), bf16[32,3,112,128]{3,2,1,0:T(8,128)(2,1)S(1)}, u32[]{:S(2)}, u32[]{:S(2)}) async-start(bf16[32,3,112,128]{3,2,1,0:T(8,128)(2,1)} %bitcast.2), calls=%async_computation.1 | async-start | bytes 5505024 | tf_op jit(solution)/shard_map/all_to_all | solution.py:486
  115.5 7.4 %collective-permute-start = (bf16[4,112,128]{2,1,0:T(8,128)(2,1)S(1)}, bf16[4,112,128]{2,1,0:T(8,128)(2,1)S(1)}, u32[]{:S(2)}, u32[]{:S(2)}) collective-permute-start(bf16[4,112,128]{2,1,0:T(8,128)(2,1)S(1)} %get-tuple-element.20), channel_id=1, source_target_pairs={{0,4},{1,5},{2,6},{3,7},{4,0},{5,1},{6,2},{7,3},{8,12},{9,13},{10,... | collective-permute-start | bytes 344072 | tf_op jit(solution)/shard_map/ppermute | solution.py:478
  115.9 10.7 %collective-permute-start.1 = (bf16[4,112,128]{2,1,0:T(8,128)(2,1)S(1)}, bf16[4,112,128]{2,1,0:T(8,128)(2,1)S(1)}, u32[]{:S(2)}, u32[]{:S(2)}) collective-permute-start(bf16[4,112,128]{2,1,0:T(8,128)(2,1)S(1)} %get-tuple-element.21), channel_id=1, source_target_pairs={{0,8},{1,9},{2,10},{3,11},{4,12},{5,13},{6,14},{7,15},{8,0},{9,1},... | collective-permute-start | bytes 344072 | tf_op jit(solution)/shard_map/ppermute | solution.py:478
  120.5 9.7 %collective-permute-start.2 = (bf16[4,112,128]{2,1,0:T(8,128)(2,1)S(1)}, bf16[4,112,128]{2,1,0:T(8,128)(2,1)S(1)}, u32[]{:S(2)}, u32[]{:S(2)}) collective-permute-start(bf16[4,112,128]{2,1,0:T(8,128)(2,1)S(1)} %get-tuple-element.22), channel_id=1, source_target_pairs={{0,12},{1,13},{2,14},{3,15},{4,8},{5,9},{6,10},{7,11},{8,4},{9,5},... | collective-permute-start | bytes 344072 | tf_op jit(solution)/shard_map/ppermute | solution.py:478
  121.0 9.2 %collective-permute-start.3 = (bf16[4,112,128]{2,1,0:T(8,128)(2,1)S(1)}, bf16[4,112,128]{2,1,0:T(8,128)(2,1)S(1)}, u32[]{:S(2)}, u32[]{:S(2)}) collective-permute-start(bf16[4,112,128]{2,1,0:T(8,128)(2,1)S(1)} %get-tuple-element.23), channel_id=1, source_target_pairs={{0,16},{1,17},{2,18},{3,19},{4,20},{5,21},{6,22},{7,23},{8,24},{9,... | collective-permute-start | bytes 344072 | tf_op jit(solution)/shard_map/ppermute | solution.py:478
  121.0 15.5 %collective-permute-start.4 = (bf16[4,112,128]{2,1,0:T(8,128)(2,1)S(1)}, bf16[4,112,128]{2,1,0:T(8,128)(2,1)S(1)}, u32[]{:S(2)}, u32[]{:S(2)}) collective-permute-start(bf16[4,112,128]{2,1,0:T(8,128)(2,1)S(1)} %get-tuple-element.24), channel_id=1, source_target_pairs={{0,20},{1,21},{2,22},{3,23},{4,16},{5,17},{6,18},{7,19},{8,28},{9,... | collective-permute-start | bytes 344072 | tf_op jit(solution)/shard_map/ppermute | solution.py:478
  123.0 13.5 %copy-start.2 = (bf16[4,112,128]{2,1,0:T(8,128)(2,1)}, bf16[4,112,128]{2,1,0:T(8,128)(2,1)S(1)}, u32[]{:S(2)}) copy-start(bf16[4,112,128]{2,1,0:T(8,128)(2,1)S(1)} %collective-permute-done.refs_1_) | copy-start | bytes 344068
  123.0 13.5 %collective-permute-start.5 = (bf16[4,112,128]{2,1,0:T(8,128)(2,1)S(1)}, bf16[4,112,128]{2,1,0:T(8,128)(2,1)S(1)}, u32[]{:S(2)}, u32[]{:S(2)}) collective-permute-start(bf16[4,112,128]{2,1,0:T(8,128)(2,1)S(1)} %get-tuple-element.25), channel_id=1, source_target_pairs={{0,24},{1,25},{2,26},{3,27},{4,28},{5,29},{6,30},{7,31},{8,16},{9,... | collective-permute-start | bytes 344072 | tf_op jit(solution)/shard_map/ppermute | solution.py:478
  126.6 9.8 %copy-start.3 = (bf16[4,112,128]{2,1,0:T(8,128)(2,1)}, bf16[4,112,128]{2,1,0:T(8,128)(2,1)S(1)}, u32[]{:S(2)}) copy-start(bf16[4,112,128]{2,1,0:T(8,128)(2,1)S(1)} %collective-permute-done.1.refs_2_) | copy-start | bytes 344068
  126.6 9.8 %collective-permute-start.6 = (bf16[4,112,128]{2,1,0:T(8,128)(2,1)S(1)}, bf16[4,112,128]{2,1,0:T(8,128)(2,1)S(1)}, u32[]{:S(2)}, u32[]{:S(2)}) collective-permute-start(bf16[4,112,128]{2,1,0:T(8,128)(2,1)S(1)} %get-tuple-element.26), channel_id=1, source_target_pairs={{0,28},{1,29},{2,30},{3,31},{4,24},{5,25},{6,26},{7,27},{8,20},{9,... | collective-permute-start | bytes 344072 | tf_op jit(solution)/shard_map/ppermute | solution.py:478
  130.2 6.3 %copy-start.4 = (bf16[4,112,128]{2,1,0:T(8,128)(2,1)}, bf16[4,112,128]{2,1,0:T(8,128)(2,1)S(1)}, u32[]{:S(2)}) copy-start(bf16[4,112,128]{2,1,0:T(8,128)(2,1)S(1)} %collective-permute-done.2.refs_3_) | copy-start | bytes 344068
  130.2 6.3 %copy-start.5 = (bf16[4,112,128]{2,1,0:T(8,128)(2,1)}, bf16[4,112,128]{2,1,0:T(8,128)(2,1)S(1)}, u32[]{:S(2)}) copy-start(bf16[4,112,128]{2,1,0:T(8,128)(2,1)S(1)} %collective-permute-done.3.refs_4_) | copy-start | bytes 344068
  136.4 0.7 copy-start.7
  136.4 0.7 copy-start.8
  139.4 52.0 %collective-permute-start.7 = (bf16[8,112,128]{2,1,0:T(8,128)(2,1)}, bf16[8,112,128]{2,1,0:T(8,128)(2,1)S(1)}, u32[]{:S(2)}, u32[]{:S(2)}) collective-permute-start(bf16[8,112,128]{2,1,0:T(8,128)(2,1)} %get-tuple-element.30), channel_id=1, source_target_pairs={{0,1},{1,2},{2,3},{3,0},{4,5},{5,6},{6,7},{7,4},{8,9},{9,10},{10,1... | collective-permute-start | bytes 688136 | tf_op jit(solution)/shard_map/ppermute | solution.py:478
  142.4 49.0 %collective-permute-start.8 = (bf16[8,112,128]{2,1,0:T(8,128)(2,1)}, bf16[8,112,128]{2,1,0:T(8,128)(2,1)S(1)}, u32[]{:S(2)}, u32[]{:S(2)}) collective-permute-start(bf16[8,112,128]{2,1,0:T(8,128)(2,1)} %get-tuple-element.31), channel_id=1, source_target_pairs={{0,2},{1,3},{2,0},{3,1},{4,6},{5,7},{6,4},{7,5},{8,10},{9,11},{10,... | collective-permute-start | bytes 688136 | tf_op jit(solution)/shard_map/ppermute | solution.py:478
  143.6 47.8 %collective-permute-start.9 = (bf16[8,112,128]{2,1,0:T(8,128)(2,1)}, bf16[8,112,128]{2,1,0:T(8,128)(2,1)S(1)}, u32[]{:S(2)}, u32[]{:S(2)}) collective-permute-start(bf16[8,112,128]{2,1,0:T(8,128)(2,1)} %get-tuple-element.32), channel_id=1, source_target_pairs={{0,3},{1,0},{2,1},{3,2},{4,7},{5,4},{6,5},{7,6},{8,11},{9,8},{10,9... | collective-permute-start | bytes 688136 | tf_op jit(solution)/shard_map/ppermute | solution.py:478
  184.5 0.9 copy-start
  185.4 28.6 %all-to-all-start.2 = ((bf16[32,112,128]{2,1,0:T(8,128)(2,1)}), bf16[32,112,128]{2,1,0:T(8,128)(2,1)}, u32[]{:S(2)}, u32[]{:S(2)}) async-start(bf16[32,112,128]{2,1,0:T(8,128)(2,1)} %copy-done), calls=%async_computation.2 | async-start | bytes 1835008 | tf_op jit(solution)/shard_map/all_to_all | solution.py:495
  191.4 0.7 copy-start.9
  191.4 0.8 copy-start.10
  191.4 0.8 copy-start.11
  (2 other events, 1.3 us)
